TPU v7x, 32 devices: a whole 2x2x4 slice. The times are simulated.
32 devices in a mesh: groups: 2 (over y), lat: 4 (over z), lon: 2 (over x), ens: 2 (over core).
Axes of the slice: x: 2, y: 2, z: 4, core: 2. Of those that a mesh axis runs over, the one named last changes fastest.
Arguments:
- fields: bfloat16 [4, 8, 1440, 384], P(('groups', 'ens'), 'lat', 'lon'), parts along dimension 0, may hold values from -6 to 6
- cotangent: bfloat16 [4, 8, 1440, 384], P(('groups', 'ens'), 'lat', 'lon'), parts along dimension 0, may hold values from -6 to 6
- filter_one: bfloat16 [8, 3, 9, 9], replicated, may hold values from -1.25 to 1.25
- filter_two: bfloat16 [8, 3, 9, 9], replicated, may hold values from -1.25 to 1.25
- mix_one: bfloat16 [432, 384], replicated, may hold values from -0.3125 to 0.3125
- mix_two: bfloat16 [432, 384], replicated, may hold values from -0.3125 to 0.3125
- source_rows: int32 [8, 3], replicated, may hold values from 0 to 7, as said below
- band_width: int32 [8, 3], replicated, may hold values from 1 to 4, as said below
Outputs:
- forward: bfloat16 [4, 8, 1440, 384], P(('groups', 'ens'), 'lat', 'lon'), parts along dimension 0
- adjoint: bfloat16 [4, 8, 1440, 384], P(('groups', 'ens'), 'lat', 'lon'), parts along dimension 0
- grad_one: float32 [864, 384], P('groups'), parts along dimension 0
- grad_two: float32 [864, 384], P('groups'), parts along dimension 0
There are 2 independent parts, one for each index of `groups`. A program takes and returns all parts, laid end to end along the dimension named above; an argument that names none is the same for every part. Nothing has to cross between parts.
Inputs may be any that keep to these rules, and one draw needn't show every extreme that they name: `source_rows`: row i lists i itself, then a row at most 2 below it and a row at most 2 above it, each clipped to the band; the distance 2 occurs. `band_width`: rows within 2 of either end of the band use the full half-width.
All inputs are finite; a program needn't handle non-finite values.
Results may differ from a plain program's by a relative error of at most 0.0067.
Values may be sent and summed in bfloat16 or wider, within the bound.
A program may use at most 192 MiB of HBM per device.

v0:
```python
import functools

import jax
import jax.numpy as jnp
from jax import lax
from jax.experimental import pallas as pl
from jax.experimental.pallas import tpu as pltpu
from jax.sharding import PartitionSpec as P

K = 9
G = 8
HALO_R = 2
WHALF = 4
WIN = 9
ROWS = 2
NEAR = 2 * HALO_R + 1
TILE = 32
SPAN = TILE + 16
HALF = 256
MARGIN = 16

F32 = jnp.float32
BF16 = jnp.bfloat16


def layer_kernel(mode, width, cols, with_mix, with_grad, *refs):
    refs = list(refs)
    up, own, down, band = refs[:4]
    refs = refs[4:]
    if with_mix:
        weights = refs[:2]
        refs = refs[2:]
    if mode == "scale":
        slope_in = refs.pop(0)
    if with_grad:
        grad_t = refs.pop(0)
    lows, highs = refs[-2:]
    refs = refs[:-2]
    rows = [up.at[0], up.at[1], own.at[0], own.at[1], down.at[0], down.at[1]]

    def basis(b, carry):
        start = pl.multiple_of(b * TILE, TILE)
        for r in range(ROWS):
            slab = jnp.concatenate(
                [rows[r + e][pl.ds(start, SPAN), :] for e in range(NEAR)], axis=0
            )
            out = jnp.dot(band[r], slab, preferred_element_type=F32).astype(BF16)
            at = pl.multiple_of(r * width + start, TILE)
            for k in range(K):
                piece = out[k * TILE : (k + 1) * TILE]
                lows[pl.ds(at, TILE), k * HALF : (k + 1) * HALF] = piece[:, :HALF]
                highs[pl.ds(at, TILE), k * HALF : (k + 1) * HALF] = piece[:, 128:]
        return carry

    lax.fori_loop(0, width // TILE, basis, 0)

    if with_mix:
        step = width // 2

        def mix(r, carry):
            for part in range(2):
                at = pl.multiple_of(r * width + part * step, 16)
                low = jnp.dot(lows[pl.ds(at, step), :], weights[0][...], preferred_element_type=F32)
                high = jnp.dot(highs[pl.ds(at, step), :], weights[1][...], preferred_element_type=F32)
                total = jnp.concatenate(
                    [low[:, :128], low[:, 128:] + high[:, :128], high[:, 128:]], axis=1
                )
                span = slice(part * step, (part + 1) * step)
                if mode == "gate":
                    gate = jax.nn.sigmoid(total)
                    refs[0][r, span, :] = (total * gate).astype(BF16)
                    refs[1][r, span, :] = gate * (1.0 + total * (1.0 - gate))
                elif mode == "scale":
                    refs[0][r, span, :] = (total * slope_in[r, span, :]).astype(BF16)
                else:
                    keep = min(step, cols - part * step)
                    refs[0][r, part * step : part * step + keep, :] = total[:keep].astype(BF16)
            if mode != "plain":
                refs[0][r, width : width + MARGIN, :] = jnp.zeros((MARGIN, total.shape[1]), BF16)
            return carry

        lax.fori_loop(0, ROWS, mix, 0)

    if with_grad:
        out = refs[-1]
        depth = lows.shape[0]
        tail = depth - ROWS * width
        if tail:
            lows[ROWS * width :, :] = jnp.zeros((tail, K * HALF), BF16)
            highs[ROWS * width :, :] = jnp.zeros((tail, K * HALF), BF16)
        cg = out.shape[1] // G

        def grad(k, carry):
            at = pl.multiple_of(k * HALF, HALF)
            low = jnp.dot(grad_t[0:HALF, :], lows[:, pl.ds(at, HALF)], preferred_element_type=F32).T
            high = jnp.dot(grad_t[128:, :], highs[:, pl.ds(at, HALF)], preferred_element_type=F32).T
            lane = lax.broadcasted_iota(jnp.int32, (cg, HALF), 1)
            sums = []
            for block, base, groups in ((low, 0, range(4)), (high, 128, range(4, 8))):
                total = jnp.zeros((cg, HALF), F32)
                for g in groups:
                    first = g * cg - base
                    inside = (lane >= first) & (lane < first + cg)
                    total = total + jnp.where(inside, block[first : first + cg], 0.0)
                sums.append(total)
            low, high = sums
            out[pl.ds(pl.multiple_of(k * cg, 8), cg), :] = jnp.concatenate(
                [low[:, :128], low[:, 128:] + high[:, :128], high[:, 128:]], axis=1
            )
            return carry

        lax.fori_loop(0, K, grad, 0)


def layer(mode, cols, halo, band, weights=None, slope=None, grad_t=None):
    chan = halo[1].shape[2]
    width = halo[1].shape[1] - MARGIN
    with_mix, with_grad = weights is not None, grad_t is not None
    args = list(halo) + [band]
    outs = []
    if with_mix:
        args += list(weights)
        held = width + MARGIN if mode != "plain" else cols
        outs.append(jax.ShapeDtypeStruct((ROWS, held, chan), BF16))
    if mode == "gate":
        outs.append(jax.ShapeDtypeStruct((ROWS, width, chan), F32))
    if mode == "scale":
        args.append(slope)
    depth = ROWS * width
    if with_grad:
        args.append(grad_t)
        depth = grad_t.shape[1]
        outs.append(jax.ShapeDtypeStruct((K * chan // G, chan), F32))
    vmem = pl.BlockSpec(memory_space=pltpu.VMEM)
    flops = 2 * ROWS * width * K * HALF * 2 * HALF * (1 + with_mix + with_grad)
    return pl.pallas_call(
        functools.partial(layer_kernel, mode, width, cols, with_mix, with_grad),
        out_shape=tuple(outs),
        in_specs=[vmem] * len(args),
        out_specs=tuple([vmem] * len(outs)),
        scratch_shapes=[pltpu.VMEM((depth, K * HALF), BF16)] * 2,
        compiler_params=pltpu.CompilerParams(vmem_limit_bytes=48 * 2**20),
        cost_estimate=pl.CostEstimate(flops=flops, bytes_accessed=10 * 2**20, transcendentals=0),
    )(*args)


def exchanged(block):
    count = lax.axis_size("lat")
    up = lax.ppermute(block, "lat", [(i, i + 1) for i in range(count - 1)])
    down = lax.ppermute(block, "lat", [(i + 1, i) for i in range(count - 1)])
    return up, block, down


def masked_filters(filt, band_width):
    offsets = jnp.abs(jnp.arange(WIN, dtype=jnp.int32) - WHALF)
    keep = offsets[None, None, :] <= band_width[:, :, None]
    return filt * keep[:, :, None, :].astype(filt.dtype)


def banded(table):
    chosen = (
        jnp.arange(SPAN)[None, None, :] - jnp.arange(TILE)[None, :, None]
        == jnp.arange(WIN)[:, None, None]
    ).astype(BF16)
    out = jnp.einsum("rekw,wtv->rktev", table, chosen, preferred_element_type=F32)
    return out.astype(BF16).reshape(ROWS, K * TILE, NEAR * SPAN)


def filter_tables(kernel, source_rows, first_row):
    pad = HALO_R
    near = jnp.arange(NEAR)
    kernel = jnp.pad(kernel.astype(F32), ((pad, pad), (0, 0), (0, 0), (0, 0)))
    src = jnp.pad(source_rows, ((pad, pad), (0, 0)), constant_values=-1)
    kernel = lax.dynamic_slice_in_dim(kernel, first_row, ROWS + 2 * pad, 0)
    src = lax.dynamic_slice_in_dim(src, first_row, ROWS + 2 * pad, 0)
    own = first_row + jnp.arange(ROWS)
    hit = src[pad : pad + ROWS, :, None] == own[:, None, None] - pad + near
    pull = jnp.einsum("rse,rskw->rekw", hit.astype(F32), kernel[pad : pad + ROWS], precision="highest")
    stack = jnp.stack([kernel[r : r + NEAR] for r in range(ROWS)])
    hit = jnp.stack([src[r : r + NEAR] == own[r] for r in range(ROWS)])
    push = jnp.sum(jnp.where(hit[:, :, :, None, None], stack, 0.0), axis=2)
    return banded(pull.astype(BF16)), banded(jnp.flip(push, 3).astype(BF16))


def dense_mix(weights):
    chan = weights.shape[1]
    cg = chan // G
    tiled = jnp.broadcast_to(weights.reshape(K, 1, cg, chan), (K, G, cg, chan)).reshape(K, chan, chan)
    group = jnp.arange(chan) // cg
    same = group[:, None] == group[None, :]
    wide = jnp.where(same[None], tiled, 0).astype(BF16)
    turned = jnp.swapaxes(wide, 1, 2)
    first = (jnp.arange(chan) < chan // 2)[None, None, :]

    def windows(block):
        low = jnp.where(first, block, 0)[:, :HALF, :HALF]
        high = jnp.where(first, 0, block)[:, chan - HALF :, chan - HALF :]
        return low.reshape(K * HALF, HALF), high.reshape(K * HALF, HALF)

    return windows(wide), windows(turned)


def turned_grad(grad, width, shift):
    chan = grad.shape[2]
    cols = grad.shape[1]
    grad = jnp.pad(grad, ((0, 0), (shift, width - shift - cols), (0, 0)))
    depth = -(-ROWS * width // 256) * 256
    flat = jnp.pad(grad.reshape(ROWS * width, chan), ((0, depth - ROWS * width), (0, 0)))
    return flat.T


def shards(fields, cotangent, filter_one, filter_two, mix_one, mix_two, source_rows, band_width):
    activ = fields[0]
    cot = cotangent[0]
    cols = activ.shape[1]
    wide = 2 * WHALF
    width = -(-(cols + wide) // TILE) * TILE
    total_rows = ROWS * lax.axis_size("lat")
    total_cols = cols * lax.axis_size("lon")
    first_row = lax.axis_index("lat") * ROWS

    lon = lax.axis_size("lon")
    both = jnp.stack([activ, cot])
    left = lax.ppermute(both[:, :, cols - wide :], "lon", [(i, (i + 1) % lon) for i in range(lon)])
    right = lax.ppermute(both[:, :, :wide], "lon", [((i + 1) % lon, i) for i in range(lon)])

    def widened(index, block):
        tail = jnp.zeros((ROWS, width + MARGIN - cols - 2 * wide, block.shape[2]), BF16)
        return jnp.concatenate([left[index], block, right[index], tail], axis=1)

    fields_halo = exchanged(widened(0, activ))
    cot_wide = widened(1, cot)
    cot_halo = exchanged(cot_wide)

    pull_one, push_one = filter_tables(masked_filters(filter_one, band_width), source_rows, first_row)
    pull_two, push_two = filter_tables(masked_filters(filter_two, band_width), source_rows, first_row)
    mix_one_f, mix_one_t = dense_mix(mix_one)
    mix_two_f, mix_two_t = dense_mix(mix_two)
    cot_t = turned_grad(cot, width, 0)

    hidden, slope = layer("gate", cols, fields_halo, pull_one, mix_one_f)
    hidden_halo = exchanged(hidden)
    (pre_grad,) = layer("scale", cols, cot_halo, push_two, mix_two_t, slope=slope)
    pre_halo = exchanged(pre_grad)
    pre_t = turned_grad(pre_grad[:, WHALF : WHALF + cols], width, WHALF)
    (part_one,) = layer("none", cols, fields_halo, pull_one, grad_t=pre_t)
    forward, part_two = layer("plain", cols, hidden_halo, pull_two, mix_two_f, grad_t=cot_t)
    (adjoint,) = layer("plain", cols, pre_halo, push_one, mix_one_t)

    factor = 1.0 / jnp.sqrt(jnp.float32(total_rows * total_cols * lax.axis_size("ens")))
    total_one = lax.psum(part_one, ("lat", "lon", "ens"))
    total_two = lax.psum(part_two, ("lat", "lon", "ens"))
    return forward[None], adjoint[None], total_one * factor, total_two * factor


def solution(mesh):
    field = P(("groups", "ens"), "lat", "lon", None)
    return jax.shard_map(
        shards,
        mesh=mesh,
        in_specs=(field, field, P(), P(), P(), P(), P(), P()),
        out_specs=(field, field, P("groups", None), P("groups", None)),
        check_vma=False,
    )
```

profile of v0, /device:TPU:0, one launch (start us, length us, event | category | flops | bytes accessed | tf_op | source)
XLA Modules:
  0.0 258.8 jit_solution(11485591581600460718)
XLA Ops:
  9.0 3.0 %collective-permute-start = (bf16[2,2,8,384]{3,2,1,0:T(8,128)(2,1)S(1)}, bf16[2,2,8,384]{3,2,1,0:T(8,128)(2,1)S(1)}, u32[]{:S(2)}, u32[]{:S(2)}) collective-permute-start(bf16[2,2,8,384]{3,2,1,0:T(8,128)(2,1)S(1)} %get-tuple-element.20), channel_id=1, source_target_pairs={{0,2},{2,0},{1,3},{3,1},{4,6},{6,4},{5,7},{7,5},{8,10},{10,8},{9,1... | collective-permute-start | bytes 73736 | tf_op jit(solution)/shard_map/ppermute | solution.py:224
  16.1 1.6 fusion.2
  18.0 1.5 fusion
  22.2 5.0 %collective-permute-start.2 = (bf16[2,752,384]{2,1,0:T(8,128)(2,1)S(1)}, bf16[2,752,384]{2,1,0:T(8,128)(2,1)}, u32[]{:S(2)}, u32[]{:S(2)}) collective-permute-start(bf16[2,752,384]{2,1,0:T(8,128)(2,1)S(1)} %get-tuple-element.44.refs_1_), channel_id=1, source_target_pairs={{0,4},{4,8},{8,12},{1,5},{5,9},{9,13},{2,6},{6,10},{10,14},{3,7},{... | collective-permute-start | bytes 3465224 | tf_op jit(solution)/shard_map/ppermute | solution.py:149
  29.8 1.6 fusion.1
  32.5 5.6 %collective-permute-start.6 = (bf16[2,752,384]{2,1,0:T(8,128)(2,1)}, bf16[2,752,384]{2,1,0:T(8,128)(2,1)}, u32[]{:S(2)}, u32[]{:S(2)}) collective-permute-start(bf16[2,752,384]{2,1,0:T(8,128)(2,1)} %get-tuple-element.43.refs_1_), channel_id=1, source_target_pairs={{0,4},{4,8},{8,12},{1,5},{5,9},{9,13},{2,6},{6,10},{10,14},{3,7},{... | collective-permute-start | bytes 3465224 | tf_op jit(solution)/shard_map/ppermute | solution.py:149
  41.5 2.6 reshape.180.refs_3_
  45.5 2.6 reshape.171.refs_3_
  48.0 5.6 %select_bitcast_fusion = (bf16[9,384,384]{1,2,0:T(8,128)(2,1)}, bf16[9,384,384]{1,2,0:T(8,128)(2,1)}, bf16[9,384,384]{2,1,0:T(8,128)(2,1)}, bf16[9,384,384]{2,1,...) fusion(pred[384]{0:T(512)(128)(4,1)S(1)} %iota_compare_fusion.1, ...), kind=kLoop, calls=%fused_computation.2 | loop fusion | flops 7962624 | bytes 16736640 | tf_op jit(solution)/shard_map/jit(_where)/select_n | solution.py:197
  55.8 1.6 copy.72
  57.4 1.6 copy.64
  61.3 4.2 %slice_select_fusion.2 = (bf16[9,256,256]{2,1,0:T(8,128)(2,1)}, bf16[9,256,256]{2,1,0:T(8,128)(2,1)S(1)}, bf16[9,256,256]{2,1,0:T(8,128)(2,1)S(1)}, bf16[9,256,256]{2,1,0:T(8,128)(2,1)}) fusion(bf16[9,384,384]{2,1,0:T(8,128)(2,1)} %get-tuple-element.26, pred[256]{0:T(512)(128)(4,1)} %get-tuple-element.49, pred[256]{0:T(512)(128)(4,1)} %get-tuple-element.50, ...), kind=kLoop, calls=%fused_computation.16 | loop fusion | flops 2359296 | bytes 9437696 | tf_op jit(solution)/shard_map/jit(_where)/select_n | solution.py:197
  65.5 15.3 %shard_map.111 = (bf16[2,752,384]{2,1,0:T(8,128)(2,1)}, f32[2,736,384]{2,1,0:T(8,128)}) custom-call(bf16[2,752,384]{2,1,0:T(8,128)(2,1)} %collective-permute-done.2.refs_0_, bf16[2,752,384]{2,1,0:T(8,128)(2,1)S(1)} %get-tuple-element.44.refs_1_, bf16[2,752,384]{2,1,0:T(8,128)(2,1)} %collective-permute-done.3.refs_2_, bf16[2,288,240]{2,1,0:T(8,128)(2,1)S(1)} %copy-done, ...), custom_call_target="tpu_custom_call" | custom-call | flops 6945767424 | bytes 10485760 | tf_op jit(solution)/shard_map/pallas_call | solution.py:136
  80.7 5.6 %collective-permute-start.4 = (bf16[2,752,384]{2,1,0:T(8,128)(2,1)}, bf16[2,752,384]{2,1,0:T(8,128)(2,1)}, u32[]{:S(2)}, u32[]{:S(2)}) collective-permute-start(bf16[2,752,384]{2,1,0:T(8,128)(2,1)} %get-tuple-element.8.refs_1_), channel_id=1, source_target_pairs={{0,4},{4,8},{8,12},{1,5},{5,9},{9,13},{2,6},{6,10},{10,14},{3,7},{... | collective-permute-start | bytes 3465224 | tf_op jit(solution)/shard_map/ppermute | solution.py:149
  87.7 15.3 %shard_map.113.refs_1_ = bf16[2,752,384]{2,1,0:T(8,128)(2,1)} custom-call(bf16[2,752,384]{2,1,0:T(8,128)(2,1)} %collective-permute-done.6.refs_0_, bf16[2,752,384]{2,1,0:T(8,128)(2,1)} %get-tuple-element.43.refs_1_, bf16[2,752,384]{2,1,0:T(8,128)(2,1)} %collective-permute-done.7.refs_2_, bf16[2,288,240]{2,1,0:T(8,128)(2,1)S(1)} %copy-done.3, ...), custom_call_target="tpu_custom_call" | custom-call | flops 6945767424 | bytes 10485760 | tf_op jit(solution)/shard_map/pallas_call | solution.py:136
  104.5 5.5 %collective-permute-start.8 = (bf16[2,752,384]{2,1,0:T(8,128)(2,1)}, bf16[2,752,384]{2,1,0:T(8,128)(2,1)}, u32[]{:S(2)}, u32[]{:S(2)}) collective-permute-start(bf16[2,752,384]{2,1,0:T(8,128)(2,1)} %shard_map.113.refs_1_), channel_id=1, source_target_pairs={{0,4},{4,8},{8,12},{1,5},{5,9},{9,13},{2,6},{6,10},{10,14},{3,7},{... | collective-permute-start | bytes 3465224 | tf_op jit(solution)/shard_map/ppermute | solution.py:149
  112.8 1.6 copy.79
  115.4 16.3 %shard_map.115 = f32[432,384]{1,0:T(8,128)} custom-call(bf16[2,752,384]{2,1,0:T(8,128)(2,1)} %collective-permute-done.2.refs_0_, bf16[2,752,384]{2,1,0:T(8,128)(2,1)S(1)} %get-tuple-element.44.refs_1_, bf16[2,752,384]{2,1,0:T(8,128)(2,1)} %collective-permute-done.3.refs_2_, bf16[2,288,240]{2,1,0:T(8,128)(2,1)S(1)} %copy-done.1, ...), custom_call_target="tpu_custom_call" | custom-call | flops 6945767424 | bytes 10485760 | tf_op jit(solution)/shard_map/pallas_call | solution.py:136
  131.7 21.2 %shard_map.112 = (bf16[2,720,384]{2,1,0:T(8,128)(2,1)}, f32[432,384]{1,0:T(8,128)}) custom-call(bf16[2,752,384]{2,1,0:T(8,128)(2,1)} %collective-permute-done.4.refs_0_, bf16[2,752,384]{2,1,0:T(8,128)(2,1)} %get-tuple-element.8.refs_1_, bf16[2,752,384]{2,1,0:T(8,128)(2,1)} %collective-permute-done.5.refs_2_, bf16[2,288,240]{2,1,0:T(8,128)(2,1)S(1)} %copy-done.2, ...), custom_call_target="tpu_custom_call" | custom-call | flops 10418651136 | bytes 10485760 | tf_op jit(solution)/shard_map/pallas_call | solution.py:136
  156.4 2.4 slice.130
  158.8 1.6 copy.78
  160.4 14.2 %shard_map.114 = bf16[2,720,384]{2,1,0:T(8,128)(2,1)} custom-call(bf16[2,752,384]{2,1,0:T(8,128)(2,1)} %collective-permute-done.8.refs_0_, bf16[2,752,384]{2,1,0:T(8,128)(2,1)} %shard_map.113.refs_1_, bf16[2,752,384]{2,1,0:T(8,128)(2,1)} %collective-permute-done.9.refs_2_, bf16[2,288,240]{2,1,0:T(8,128)(2,1)S(1)} %reshape.183.refs_3_, ...), custom_call_target="tpu_custom_call" | custom-call | flops 6945767424 | bytes 10485760 | tf_op jit(solution)/shard_map/pallas_call | solution.py:136
  174.5 74.4 %all-reduce.10.cloned.1.call-done = (f32[432,384]{1,0:T(8,128)}, f32[432,384]{1,0:T(8,128)}) async-done(((f32[432,384]{1,0:T(8,128)}, f32[432,384]{1,0:T(8,128)}), (f32[432,384]{1,0:T(8,128)}, f32[432,384]{1,0:T(8,128)})) %all-reduce.10.cloned.1.call-update) | async-done | bytes 1327120 | tf_op jit(solution)/shard_map/psum | solution.py:251
  249.0 2.1 broadcast_multiply_fusion
  (103 shorter events, 32.6 us)
Async XLA Ops:
  7.2 241.8 %all-reduce.10.cloned.1.call-start = ((), (), s32[]{:S(2)}) async-start(), calls=%async_computation | async-start | bytes 2654208 | tf_op jit(solution)/shard_map/psum | solution.py:251
  8.7 4.0 %copy-start.15 = (s32[8,3]{0,1:T(4,128)S(1)}, s32[8,3]{0,1:T(4,128)}, u32[]{:S(2)}) copy-start(s32[8,3]{0,1:T(4,128)} %param.14) | copy-start | bytes 292
  8.7 5.6 %copy-start.14 = (s32[8,3]{0,1:T(4,128)S(1)}, s32[8,3]{0,1:T(4,128)}, u32[]{:S(2)}) copy-start(s32[8,3]{0,1:T(4,128)} %param.15) | copy-start | bytes 292
  8.7 5.8 %copy-start.12 = (bf16[8,3,9,9]{3,0,2,1:T(8,128)(2,1)S(1)}, bf16[8,3,9,9]{3,0,2,1:T(8,128)(2,1)}, u32[]{:S(2)}) copy-start(bf16[8,3,9,9]{3,0,2,1:T(8,128)(2,1)} %param.11) | copy-start | bytes 11668
  8.7 5.8 %copy-start.13 = (bf16[8,3,9,9]{3,0,2,1:T(8,128)(2,1)S(1)}, bf16[8,3,9,9]{3,0,2,1:T(8,128)(2,1)}, u32[]{:S(2)}) copy-start(bf16[8,3,9,9]{3,0,2,1:T(8,128)(2,1)} %param.10) | copy-start | bytes 11668
  9.0 11.7 %collective-permute-start = (bf16[2,2,8,384]{3,2,1,0:T(8,128)(2,1)S(1)}, bf16[2,2,8,384]{3,2,1,0:T(8,128)(2,1)S(1)}, u32[]{:S(2)}, u32[]{:S(2)}) collective-permute-start(bf16[2,2,8,384]{3,2,1,0:T(8,128)(2,1)S(1)} %get-tuple-element.20), channel_id=1, source_target_pairs={{0,2},{2,0},{1,3},{3,1},{4,6},{6,4},{5,7},{7,5},{8,10},{10,8},{9,1... | collective-permute-start | bytes 73736 | tf_op jit(solution)/shard_map/ppermute | solution.py:224
  12.0 8.7 %collective-permute-start.1 = (bf16[2,2,8,384]{3,2,1,0:T(8,128)(2,1)S(1)}, bf16[2,2,8,384]{3,2,1,0:T(8,128)(2,1)S(1)}, u32[]{:S(2)}, u32[]{:S(2)}) collective-permute-start(bf16[2,2,8,384]{3,2,1,0:T(8,128)(2,1)S(1)} %get-tuple-element.21), channel_id=1, source_target_pairs={{2,0},{0,2},{3,1},{1,3},{6,4},{4,6},{7,5},{5,7},{10,8},{8,10},{11,... | collective-permute-start | bytes 73736 | tf_op jit(solution)/shard_map/ppermute | solution.py:225
  17.7 3.0 %copy-start.7 = (bf16[1,2,720,384]{3,2,1,0:T(8,128)(2,1)S(1)}, bf16[1,2,720,384]{3,2,1,0:T(8,128)(2,1)}, u32[]{:S(2)}) copy-start(bf16[1,2,720,384]{3,2,1,0:T(8,128)(2,1)} %param.8) | copy-start | bytes 3317764
  22.2 43.3 %collective-permute-start.2 = (bf16[2,752,384]{2,1,0:T(8,128)(2,1)S(1)}, bf16[2,752,384]{2,1,0:T(8,128)(2,1)}, u32[]{:S(2)}, u32[]{:S(2)}) collective-permute-start(bf16[2,752,384]{2,1,0:T(8,128)(2,1)S(1)} %get-tuple-element.44.refs_1_), channel_id=1, source_target_pairs={{0,4},{4,8},{8,12},{1,5},{5,9},{9,13},{2,6},{6,10},{10,14},{3,7},{... | collective-permute-start | bytes 3465224 | tf_op jit(solution)/shard_map/ppermute | solution.py:149
  27.2 38.3 %collective-permute-start.3 = (bf16[2,752,384]{2,1,0:T(8,128)(2,1)S(1)}, bf16[2,752,384]{2,1,0:T(8,128)(2,1)}, u32[]{:S(2)}, u32[]{:S(2)}) collective-permute-start(bf16[2,752,384]{2,1,0:T(8,128)(2,1)S(1)} %get-tuple-element.44.refs_1_), channel_id=1, source_target_pairs={{4,0},{8,4},{12,8},{5,1},{9,5},{13,9},{6,2},{10,6},{14,10},{7,3},{... | collective-permute-start | bytes 3465224 | tf_op jit(solution)/shard_map/ppermute | solution.py:150
  31.4 8.8 %copy-start.5 = (bf16[2,9,32,5,48]{4,1,3,0,2:T(8,128)(2,1)S(1)}, bf16[2,9,32,5,48]{4,1,3,0,2:T(8,128)(2,1)}, u32[]{:S(2)}) copy-start(bf16[2,9,32,5,48]{4,1,3,0,2:T(8,128)(2,1)} %fusion.2) | copy-start | bytes 829444
  32.5 55.1 %collective-permute-start.6 = (bf16[2,752,384]{2,1,0:T(8,128)(2,1)}, bf16[2,752,384]{2,1,0:T(8,128)(2,1)}, u32[]{:S(2)}, u32[]{:S(2)}) collective-permute-start(bf16[2,752,384]{2,1,0:T(8,128)(2,1)} %get-tuple-element.43.refs_1_), channel_id=1, source_target_pairs={{0,4},{4,8},{8,12},{1,5},{5,9},{9,13},{2,6},{6,10},{10,14},{3,7},{... | collective-permute-start | bytes 3465224 | tf_op jit(solution)/shard_map/ppermute | solution.py:149
  38.1 49.6 %collective-permute-start.7 = (bf16[2,752,384]{2,1,0:T(8,128)(2,1)}, bf16[2,752,384]{2,1,0:T(8,128)(2,1)}, u32[]{:S(2)}, u32[]{:S(2)}) collective-permute-start(bf16[2,752,384]{2,1,0:T(8,128)(2,1)} %get-tuple-element.43.refs_1_), channel_id=1, source_target_pairs={{4,0},{8,4},{12,8},{5,1},{9,5},{13,9},{6,2},{10,6},{14,10},{7,3},{... | collective-permute-start | bytes 3465224 | tf_op jit(solution)/shard_map/ppermute | solution.py:150
  41.5 2.6 copy-start.6
  45.5 2.6 copy-start.9
  45.5 2.6 copy-start.10
  45.5 2.6 copy-start.11
  61.3 4.2 %copy-start = (bf16[2,288,240]{2,1,0:T(8,128)(2,1)S(1)}, bf16[2,288,240]{2,1,0:T(8,128)(2,1)}, u32[]{:S(2)}) copy-start(bf16[2,288,240]{2,1,0:T(8,128)(2,1)} %reshape.171.refs_3_) | copy-start | bytes 829444
  65.4 22.2 %copy-start.3 = (bf16[2,288,240]{2,1,0:T(8,128)(2,1)S(1)}, bf16[2,288,240]{2,1,0:T(8,128)(2,1)}, u32[]{:S(2)}) copy-start(bf16[2,288,240]{2,1,0:T(8,128)(2,1)} %reshape.180.refs_3_) | copy-start | bytes 829444
  80.7 51.0 %collective-permute-start.4 = (bf16[2,752,384]{2,1,0:T(8,128)(2,1)}, bf16[2,752,384]{2,1,0:T(8,128)(2,1)}, u32[]{:S(2)}, u32[]{:S(2)}) collective-permute-start(bf16[2,752,384]{2,1,0:T(8,128)(2,1)} %get-tuple-element.8.refs_1_), channel_id=1, source_target_pairs={{0,4},{4,8},{8,12},{1,5},{5,9},{9,13},{2,6},{6,10},{10,14},{3,7},{... | collective-permute-start | bytes 3465224 | tf_op jit(solution)/shard_map/ppermute | solution.py:149
  86.3 45.4 %collective-permute-start.5 = (bf16[2,752,384]{2,1,0:T(8,128)(2,1)}, bf16[2,752,384]{2,1,0:T(8,128)(2,1)}, u32[]{:S(2)}, u32[]{:S(2)}) collective-permute-start(bf16[2,752,384]{2,1,0:T(8,128)(2,1)} %get-tuple-element.8.refs_1_), channel_id=1, source_target_pairs={{4,0},{8,4},{12,8},{5,1},{9,5},{13,9},{6,2},{10,6},{14,10},{7,3},{... | collective-permute-start | bytes 3465224 | tf_op jit(solution)/shard_map/ppermute | solution.py:150
  104.5 55.9 %collective-permute-start.8 = (bf16[2,752,384]{2,1,0:T(8,128)(2,1)}, bf16[2,752,384]{2,1,0:T(8,128)(2,1)}, u32[]{:S(2)}, u32[]{:S(2)}) collective-permute-start(bf16[2,752,384]{2,1,0:T(8,128)(2,1)} %shard_map.113.refs_1_), channel_id=1, source_target_pairs={{0,4},{4,8},{8,12},{1,5},{5,9},{9,13},{2,6},{6,10},{10,14},{3,7},{... | collective-permute-start | bytes 3465224 | tf_op jit(solution)/shard_map/ppermute | solution.py:149
  110.0 50.3 %collective-permute-start.9 = (bf16[2,752,384]{2,1,0:T(8,128)(2,1)}, bf16[2,752,384]{2,1,0:T(8,128)(2,1)}, u32[]{:S(2)}, u32[]{:S(2)}) collective-permute-start(bf16[2,752,384]{2,1,0:T(8,128)(2,1)} %shard_map.113.refs_1_), channel_id=1, source_target_pairs={{4,0},{8,4},{12,8},{5,1},{9,5},{13,9},{6,2},{10,6},{14,10},{7,3},{... | collective-permute-start | bytes 3465224 | tf_op jit(solution)/shard_map/ppermute | solution.py:150
  115.4 16.3 %copy-start.2 = (bf16[2,288,240]{2,1,0:T(8,128)(2,1)S(1)}, bf16[2,288,240]{2,1,0:T(8,128)(2,1)}, u32[]{:S(2)}) copy-start(bf16[2,288,240]{2,1,0:T(8,128)(2,1)} %reshape.175.refs_3_) | copy-start | bytes 829444
  (3 other events, 4.6 us)
Sparse Core Ops, SparseCore 0:
  153.1 95.8 all-reduce.9
where the time goes:
time: 260 us; the launch traced here: 259 us
  Pallas kernels  82.3 us (32%)
  waiting for transfers between devices  74.5 us (29%)
  local copies, waits for them, and re-layouts  33.9 us (13%)
  starting transfers between devices  30.3 us (12%)
  other arithmetic  17.6 us (7%)
  between operations  14.4 us (6%)
  matrix products  5.74 us (2%)
    pallas_call x5, Pallas kernels, layer(): pl.pallas_call(functools.partial(layer_kernel, mode, width, cols, with_mi...  82.3 us
    psum x1, waiting for transfers between devices, shards(): total_one = lax.psum(part_one, ('lat', 'lon', 'ens'))  74.4 us
    ppermute x4, starting transfers between devices, exchanged(): up = lax.ppermute(block, 'lat', [(i, i + 1) for i in range(count - 1)])  21.7 us
    select_n x2, other arithmetic, windows(): high = jnp.where(first, 0, block)[:, chan - HALF:, chan - HALF:]  9.74 us
    slice x5, local copies, waits for them, and re-layouts, windows(): high = jnp.where(first, 0, block)[:, chan - HALF:, chan - HALF:]  7.45 us
    reshape x4, local copies, waits for them, and re-layouts, banded(): return out.astype(BF16).reshape(ROWS, K * TILE, NEAR * SPAN)  6.96 us
    ppermute x4, starting transfers between devices, exchanged(): down = lax.ppermute(block, 'lat', [(i + 1, i) for i in range(count - 1)])  5.52 us
    dot_general x4, matrix products, banded(): jnp.einsum('rekw,wtv->rktev', table, chosen, preferred_element_type=F32)  5.21 us
  transfers between devices with their start and end apart: 11, of which 1 were waited for; matrix products, arithmetic and copies ran while one was open for 19% of the time, Pallas kernels for 32%

commit v1 on v0

--- a/solution.py
+++ b/solution.py
@@ -23,20 +23,45 @@
 BF16 = jnp.bfloat16
 
 
-def layer_kernel(mode, width, cols, with_mix, with_grad, *refs):
+def group_windows(block, cg):
+    lane = lax.broadcasted_iota(jnp.int32, (cg, block.shape[1]), 1)
+    low = [jnp.where((lane >= g * cg) & (lane < (g + 1) * cg), block, 0.0) for g in range(G)]
+    wide = jnp.concatenate(low[: G // 2], axis=0)[:, :HALF]
+    rest = jnp.concatenate(low[G // 2 :], axis=0)[:, 128:]
+    gap = jnp.zeros((HALF - wide.shape[0], HALF), F32)
+    return jnp.concatenate([wide, gap], axis=0), jnp.concatenate([gap, rest], axis=0)
+
+
+def layer_kernel(mode, width, cols, turn, valid, with_mix, with_grad, *refs):
     refs = list(refs)
     up, own, down, band = refs[:4]
     refs = refs[4:]
     if with_mix:
-        weights = refs[:2]
-        refs = refs[2:]
+        mix_ref = refs.pop(0)
     if mode == "scale":
         slope_in = refs.pop(0)
     if with_grad:
-        grad_t = refs.pop(0)
+        grad_in = refs.pop(0)
+        turned = refs.pop()
+        padded = refs.pop()
+    if with_mix:
+        weights = refs[-2:]
+        refs = refs[:-2]
     lows, highs = refs[-2:]
     refs = refs[:-2]
     rows = [up.at[0], up.at[1], own.at[0], own.at[1], down.at[0], down.at[1]]
+
+    if with_mix:
+        cg = mix_ref.shape[1] // G
+
+        def spread(k, carry):
+            block = mix_ref[pl.ds(pl.multiple_of(k * cg, 16), cg), :].astype(F32)
+            at = pl.ds(pl.multiple_of(k * HALF, HALF), HALF)
+            for dest, window in zip(weights, group_windows(block, cg)):
+                dest[at, :] = (window.T if turn else window).astype(BF16)
+            return carry
+
+        lax.fori_loop(0, K, spread, 0)
 
     def basis(b, carry):
         start = pl.multiple_of(b * TILE, TILE)
@@ -83,17 +108,26 @@
 
     if with_grad:
         out = refs[-1]
-        depth = lows.shape[0]
-        tail = depth - ROWS * width
-        if tail:
-            lows[ROWS * width :, :] = jnp.zeros((tail, K * HALF), BF16)
-            highs[ROWS * width :, :] = jnp.zeros((tail, K * HALF), BF16)
         cg = out.shape[1] // G
+        first, last = valid
+        size = grad_in.shape[1]
+        for r in range(ROWS):
+            padded[...] = jnp.zeros(padded.shape, F32)
+            here = min(size, width)
+            value = grad_in[r, :here, :].astype(F32)
+            place = lax.broadcasted_iota(jnp.int32, value.shape, 0)
+            padded[:here, :] = jnp.where((place >= first) & (place < last), value, 0.0)
+            turned[r] = padded[...].T.astype(BF16)
 
         def grad(k, carry):
             at = pl.multiple_of(k * HALF, HALF)
-            low = jnp.dot(grad_t[0:HALF, :], lows[:, pl.ds(at, HALF)], preferred_element_type=F32).T
-            high = jnp.dot(grad_t[128:, :], highs[:, pl.ds(at, HALF)], preferred_element_type=F32).T
+            low = jnp.zeros((HALF, HALF), F32)
+            high = jnp.zeros((HALF, HALF), F32)
+            for r in range(ROWS):
+                span = slice(r * width, (r + 1) * width)
+                low += jnp.dot(turned[r, 0:HALF, :width], lows[span, pl.ds(at, HALF)], preferred_element_type=F32)
+                high += jnp.dot(turned[r, 128:, :width], highs[span, pl.ds(at, HALF)], preferred_element_type=F32)
+            low, high = low.T, high.T
             lane = lax.broadcasted_iota(jnp.int32, (cg, HALF), 1)
             sums = []
             for block, base, groups in ((low, 0, range(4)), (high, 128, range(4, 8))):
@@ -112,14 +146,14 @@
         lax.fori_loop(0, K, grad, 0)
 
 
-def layer(mode, cols, halo, band, weights=None, slope=None, grad_t=None):
+def layer(mode, cols, halo, band, weights=None, turn=False, slope=None, grad=None, valid=None):
     chan = halo[1].shape[2]
     width = halo[1].shape[1] - MARGIN
-    with_mix, with_grad = weights is not None, grad_t is not None
+    with_mix, with_grad = weights is not None, grad is not None
     args = list(halo) + [band]
     outs = []
     if with_mix:
-        args += list(weights)
+        args.append(weights)
         held = width + MARGIN if mode != "plain" else cols
         outs.append(jax.ShapeDtypeStruct((ROWS, held, chan), BF16))
     if mode == "gate":
@@ -128,17 +162,22 @@
         args.append(slope)
     depth = ROWS * width
     if with_grad:
-        args.append(grad_t)
-        depth = grad_t.shape[1]
+        args.append(grad)
         outs.append(jax.ShapeDtypeStruct((K * chan // G, chan), F32))
+    scratch = [pltpu.VMEM((depth, K * HALF), BF16)] * 2
+    if with_mix:
+        scratch += [pltpu.VMEM((K * HALF, HALF), BF16)] * 2
+    if with_grad:
+        long = -(-width // 128) * 128
+        scratch += [pltpu.VMEM((long, chan), F32), pltpu.VMEM((ROWS, chan, long), BF16)]
     vmem = pl.BlockSpec(memory_space=pltpu.VMEM)
     flops = 2 * ROWS * width * K * HALF * 2 * HALF * (1 + with_mix + with_grad)
     return pl.pallas_call(
-        functools.partial(layer_kernel, mode, width, cols, with_mix, with_grad),
+        functools.partial(layer_kernel, mode, width, cols, turn, valid, with_mix, with_grad),
         out_shape=tuple(outs),
         in_specs=[vmem] * len(args),
         out_specs=tuple([vmem] * len(outs)),
-        scratch_shapes=[pltpu.VMEM((depth, K * HALF), BF16)] * 2,
+        scratch_shapes=scratch,
         compiler_params=pltpu.CompilerParams(vmem_limit_bytes=48 * 2**20),
         cost_estimate=pl.CostEstimate(flops=flops, bytes_accessed=10 * 2**20, transcendentals=0),
     )(*args)
@@ -182,31 +221,108 @@
     return banded(pull.astype(BF16)), banded(jnp.flip(push, 3).astype(BF16))
 
 
-def dense_mix(weights):
-    chan = weights.shape[1]
-    cg = chan // G
-    tiled = jnp.broadcast_to(weights.reshape(K, 1, cg, chan), (K, G, cg, chan)).reshape(K, chan, chan)
-    group = jnp.arange(chan) // cg
-    same = group[:, None] == group[None, :]
-    wide = jnp.where(same[None], tiled, 0).astype(BF16)
-    turned = jnp.swapaxes(wide, 1, 2)
-    first = (jnp.arange(chan) < chan // 2)[None, None, :]
-
-    def windows(block):
-        low = jnp.where(first, block, 0)[:, :HALF, :HALF]
-        high = jnp.where(first, 0, block)[:, chan - HALF :, chan - HALF :]
-        return low.reshape(K * HALF, HALF), high.reshape(K * HALF, HALF)
-
-    return windows(wide), windows(turned)
-
-
-def turned_grad(grad, width, shift):
-    chan = grad.shape[2]
-    cols = grad.shape[1]
-    grad = jnp.pad(grad, ((0, 0), (shift, width - shift - cols), (0, 0)))
-    depth = -(-ROWS * width // 256) * 256
-    flat = jnp.pad(grad.reshape(ROWS * width, chan), ((0, depth - ROWS * width), (0, 0)))
-    return flat.T
+def sum_kernel(axes, sizes, total, part, result, *scratch):
+    slots = scratch[: len(axes)]
+    send_sem, recv_sem = scratch[len(axes) :]
+    places = [lax.axis_index(axis) for axis in axes]
+    barrier = pltpu.get_barrier_semaphore()
+    greeted = 0
+    for axis, size, place in zip(axes, sizes, places):
+        for d in range(1, size):
+            peer = lax.rem(place + d, size)
+            pl.semaphore_signal(barrier, inc=1, device_id={axis: peer}, device_id_type=pl.DeviceIdType.MESH)
+            greeted += 1
+    pl.semaphore_wait(barrier, greeted)
+
+    used = 0
+    base, extent = 0, total
+    bases = []
+
+    def block(ref, start, count):
+        return ref.at[pl.ds(pl.multiple_of(start, 8), count)]
+
+    for level, (axis, size, place) in enumerate(zip(axes, sizes, places)):
+        bases.append((base, extent))
+        extent //= size
+        copies = []
+        for d in range(1, size):
+            peer = lax.rem(place + d, size)
+            copy = pltpu.make_async_remote_copy(
+                src_ref=block(part, base + peer * extent, extent),
+                dst_ref=slots[level].at[d - 1],
+                send_sem=send_sem.at[used],
+                recv_sem=recv_sem.at[used],
+                device_id={axis: peer},
+                device_id_type=pl.DeviceIdType.MESH,
+            )
+            copy.start()
+            copies.append(copy)
+            used += 1
+        base = base + place * extent
+        for copy in copies:
+            copy.wait()
+        mine = pl.ds(pl.multiple_of(base, 8), extent)
+        value = part[mine, :]
+        for d in range(1, size):
+            value = value + slots[level][d - 1]
+        part[mine, :] = value
+    result[mine, :] = value
+    for level in reversed(range(len(axes))):
+        axis, size, place = axes[level], sizes[level], places[level]
+        outer, whole = bases[level]
+        extent = whole // size
+        copies = []
+        for d in range(1, size):
+            peer = lax.rem(place + d, size)
+            own = outer + place * extent
+            copy = pltpu.make_async_remote_copy(
+                src_ref=block(result, own, extent),
+                dst_ref=block(result, own, extent),
+                send_sem=send_sem.at[used],
+                recv_sem=recv_sem.at[used],
+                device_id={axis: peer},
+                device_id_type=pl.DeviceIdType.MESH,
+            )
+            copy.start()
+            copies.append(copy)
+            used += 1
+        for copy in copies:
+            copy.wait()
+
+
+def summed(parts, scale):
+    axes = ("ens", "lon", "lat")
+    sizes = [lax.axis_size(axis) for axis in axes]
+    rows = sum(part.shape[0] for part in parts)
+    chan = parts[0].shape[1]
+    devices = sizes[0] * sizes[1] * sizes[2]
+    total = -(-rows // (8 * devices)) * 8 * devices
+    filler = jnp.zeros((total - rows, chan), F32)
+    stacked = jnp.concatenate([part * scale for part in parts] + [filler], axis=0)
+    slots, extent, count = [], total, 0
+    for size in sizes:
+        extent //= size
+        slots.append(pltpu.VMEM((size - 1, extent, chan), F32))
+        count += 2 * (size - 1)
+
+    def kernel(part, result, held, *scratch):
+        held[...] = part[...]
+        sum_kernel(axes, sizes, total, held, result, *scratch)
+
+    vmem = pl.BlockSpec(memory_space=pltpu.VMEM)
+    return pl.pallas_call(
+        kernel,
+        out_shape=jax.ShapeDtypeStruct((total, chan), F32),
+        in_specs=[vmem],
+        out_specs=vmem,
+        scratch_shapes=[pltpu.VMEM((total, chan), F32)]
+        + slots
+        + [pltpu.SemaphoreType.DMA((count,)), pltpu.SemaphoreType.DMA((count,))],
+        compiler_params=pltpu.CompilerParams(
+            collective_id=0, has_side_effects=True, vmem_limit_bytes=32 * 2**20
+        ),
+        cost_estimate=pl.CostEstimate(flops=0, bytes_accessed=20 * 2**20, transcendentals=0),
+    )(stacked)
 
 
 def shards(fields, cotangent, filter_one, filter_two, mix_one, mix_two, source_rows, band_width):
@@ -220,9 +336,10 @@
     first_row = lax.axis_index("lat") * ROWS
 
     lon = lax.axis_size("lon")
-    both = jnp.stack([activ, cot])
-    left = lax.ppermute(both[:, :, cols - wide :], "lon", [(i, (i + 1) % lon) for i in range(lon)])
-    right = lax.ppermute(both[:, :, :wide], "lon", [((i + 1) % lon, i) for i in range(lon)])
+    head = jnp.stack([activ[:, :wide], cot[:, :wide]])
+    tail = jnp.stack([activ[:, cols - wide :], cot[:, cols - wide :]])
+    left = lax.ppermute(tail, "lon", [(i, (i + 1) % lon) for i in range(lon)])
+    right = lax.ppermute(head, "lon", [((i + 1) % lon, i) for i in range(lon)])
 
     def widened(index, block):
         tail = jnp.zeros((ROWS, width + MARGIN - cols - 2 * wide, block.shape[2]), BF16)
@@ -234,23 +351,21 @@
 
     pull_one, push_one = filter_tables(masked_filters(filter_one, band_width), source_rows, first_row)
     pull_two, push_two = filter_tables(masked_filters(filter_two, band_width), source_rows, first_row)
-    mix_one_f, mix_one_t = dense_mix(mix_one)
-    mix_two_f, mix_two_t = dense_mix(mix_two)
-    cot_t = turned_grad(cot, width, 0)
-
-    hidden, slope = layer("gate", cols, fields_halo, pull_one, mix_one_f)
+
+    hidden, slope = layer("gate", cols, fields_halo, pull_one, mix_one)
     hidden_halo = exchanged(hidden)
-    (pre_grad,) = layer("scale", cols, cot_halo, push_two, mix_two_t, slope=slope)
+    (pre_grad,) = layer("scale", cols, cot_halo, push_two, mix_two, turn=True, slope=slope)
     pre_halo = exchanged(pre_grad)
-    pre_t = turned_grad(pre_grad[:, WHALF : WHALF + cols], width, WHALF)
-    (part_one,) = layer("none", cols, fields_halo, pull_one, grad_t=pre_t)
-    forward, part_two = layer("plain", cols, hidden_halo, pull_two, mix_two_f, grad_t=cot_t)
-    (adjoint,) = layer("plain", cols, pre_halo, push_one, mix_one_t)
+    inner = (WHALF, WHALF + cols)
+    (part_one,) = layer("none", cols, fields_halo, pull_one, grad=pre_grad, valid=inner)
+    forward, part_two = layer("plain", cols, hidden_halo, pull_two, mix_two, grad=cot, valid=(0, cols))
+    (adjoint,) = layer("plain", cols, pre_halo, push_one, mix_one, turn=True)
 
     factor = 1.0 / jnp.sqrt(jnp.float32(total_rows * total_cols * lax.axis_size("ens")))
-    total_one = lax.psum(part_one, ("lat", "lon", "ens"))
-    total_two = lax.psum(part_two, ("lat", "lon", "ens"))
-    return forward[None], adjoint[None], total_one * factor, total_two * factor
+    sums = summed([part_one, part_two], factor)
+    length = part_one.shape[0]
+    total_one, total_two = sums[:length], sums[length : 2 * length]
+    return forward[None], adjoint[None], total_one, total_two
 
 
 def solution(mesh):

time: 260 us -> 183 us (0.70)
  waiting for transfers between devices: 74.5 us -> 5.95 us
  Pallas kernels: 82.3 us -> 119 us
  between operations: 14.4 us -> 0.96 us
  other arithmetic: 17.6 us -> 5.33 us
  local copies, waits for them, and re-layouts: 33.9 us -> 24.5 us
  starting transfers between devices: 30.3 us -> 23.3 us
  matrix products: 5.74 us -> 2.49 us
    psum x1 -> x0, waiting for transfers between devices: 74.4 us -> none  [shards(): total_one = lax.psum(part_one, ('lat', 'lon', 'ens'))]
    pallas_call x5 -> x6, Pallas kernels: 82.3 us -> 119 us  [the longest x5 77.9 us: layer(): pl.pallas_call(functools.partial(layer_kernel, mode, width, cols, turn, v...]
    slice x11 -> x1, local copies, waits for them, and re-layouts: 11.9 us -> 1.14 us  [shards(): total_one, total_two = (sums[:length], sums[length:2 * length])]
    select_n x3 -> x0, other arithmetic: 9.75 us -> none  [the longest x2 9.74 us: windows(): high = jnp.where(first, 0, block)[:, chan - HALF:, chan - HALF:]]
    ppermute x4, starting transfers between devices: 21.7 us -> 14.9 us  [exchanged(): up = lax.ppermute(block, 'lat', [(i, i + 1) for i in range(count - 1)])]
    ppermute x4, waiting for transfers between devices: 0.01 us -> 5.93 us  [exchanged(): down = lax.ppermute(block, 'lat', [(i + 1, i) for i in range(count - 1)])]
    dot_general x4, matrix products: 5.21 us -> 1.96 us  [banded(): jnp.einsum('rekw,wtv->rktev', table, chosen, preferred_element_type=F32)]
    reshape x4, local copies, waits for them, and re-layouts: 6.96 us -> 9.92 us  [banded(): return out.astype(BF16).reshape(ROWS, K * TILE, NEAR * SPAN)]
  transfers between devices with their start and end apart: 11 -> 10, of which waited for: 1 -> 2; matrix products, arithmetic and copies ran while one was open for 19% -> 16% of each run, Pallas kernels for 32% -> 58%
where the time goes in v1:
time: 183 us; the launch traced here: 181 us
  Pallas kernels  119 us (65%)
  local copies, waits for them, and re-layouts  24.5 us (13%)
  starting transfers between devices  23.3 us (13%)
  waiting for transfers between devices  5.95 us (3%)
  other arithmetic  5.33 us (3%)
  matrix products  2.49 us (1%)
    pallas_call x5, Pallas kernels, layer(): pl.pallas_call(functools.partial(layer_kernel, mode, width, cols, turn, v...  77.9 us
    pallas_call x1, Pallas kernels, summed(): pl.pallas_call(kernel, out_shape=jax.ShapeDtypeStruct((total, chan), F32)...  40.9 us
    ppermute x4, starting transfers between devices, exchanged(): up = lax.ppermute(block, 'lat', [(i, i + 1) for i in range(count - 1)])  14.9 us
    reshape x4, local copies, waits for them, and re-layouts, banded(): return out.astype(BF16).reshape(ROWS, K * TILE, NEAR * SPAN)  9.92 us
    ppermute x4, waiting for transfers between devices, exchanged(): down = lax.ppermute(block, 'lat', [(i + 1, i) for i in range(count - 1)])  5.93 us
    convert_element_type x4, local copies, waits for them, and re-layouts, banded(): return out.astype(BF16).reshape(ROWS, K * TILE, NEAR * SPAN)  5.43 us
    ppermute x4, starting transfers between devices, exchanged(): down = lax.ppermute(block, 'lat', [(i + 1, i) for i in range(count - 1)])  5.32 us
    unnamed x31, local copies, waits for them, and re-layouts  3.66 us
  transfers between devices with their start and end apart: 10, of which 2 were waited for; matrix products, arithmetic and copies ran while one was open for 16% of the time, Pallas kernels for 58%

profile of v1, /device:TPU:0, one launch (start us, length us, event | category | flops | bytes accessed | tf_op | source)
XLA Modules:
  0.0 181.4 jit_solution(12922006573574458866)
XLA Ops:
  1.4 3.0 %collective-permute-start = (bf16[2,2,8,384]{3,2,1,0:T(8,128)(2,1)S(1)}, bf16[2,2,8,384]{3,2,1,0:T(8,128)(2,1)S(1)}, u32[]{:S(2)}, u32[]{:S(2)}) collective-permute-start(bf16[2,2,8,384]{3,2,1,0:T(8,128)(2,1)S(1)} %pad_maximum_fusion), channel_id=1, source_target_pairs={{0,2},{2,0},{1,3},{3,1},{4,6},{6,4},{5,7},{7,5},{8,10},{10,8},{9,1... | collective-permute-start | bytes 73736 | tf_op jit(solution)/shard_map/ppermute | solution.py:341
  10.2 1.4 fusion.33
  12.3 4.9 %collective-permute-start.2 = (bf16[2,752,384]{2,1,0:T(8,128)(2,1)S(1)}, bf16[2,752,384]{2,1,0:T(8,128)(2,1)}, u32[]{:S(2)}, u32[]{:S(2)}) collective-permute-start(bf16[2,752,384]{2,1,0:T(8,128)(2,1)S(1)} %get-tuple-element.33.refs_1_), channel_id=1, source_target_pairs={{0,4},{4,8},{8,12},{1,5},{5,9},{9,13},{2,6},{6,10},{10,14},{3,7},{... | collective-permute-start | bytes 3465224 | tf_op jit(solution)/shard_map/ppermute | solution.py:188
  18.5 1.4 copy.41
  19.9 2.5 %reshape.74.refs_3_ = bf16[2,288,240]{2,1,0:T(8,128)(2,1)} reshape(bf16[2,9,32,5,48]{4,3,2,1,0:T(8,128)(2,1)} %copy.41) | data formatting | bytes 552960 | tf_op jit(solution)/shard_map/reshape | solution.py:205
  22.5 2.0 %fusion.10 = (bf16[2,5,9,9]{3,2,1,0:T(8,128)(2,1)}, bf16[2,5,9,9]{3,2,1,0:T(8,128)(2,1)S(1)}) fusion(f32[1,5,3,9,9]{4,2,3,1,0:T(4,128)} %get-tuple-element.23, f32[1,5,3,9,9]{4,2,3,1,0:T(4,128)} %get-tuple-element.22, pred[2,5,3]{2,1,0:T(8,128)(4,1)S(1)} %copy.45, f32[1,5,3,9,9]{4,2,3,1,0:T(4,128)} %get-tuple-element.21, f32[1,5,3,9,9]{4,2,3,1,0:T(4,128)} %get-tuple-element.20), kind=kLoop, calls=%fused_computation.20 | loop fusion | flops 12960 | bytes 22710 | tf_op jit(solution)/shard_map/reduce_sum | solution.py:220
  25.1 1.4 copy.49
  26.5 2.5 %reshape.76.refs_3_ = bf16[2,288,240]{2,1,0:T(8,128)(2,1)} reshape(bf16[2,9,32,5,48]{4,3,2,1,0:T(8,128)(2,1)} %copy.49) | data formatting | bytes 552960 | tf_op jit(solution)/shard_map/reshape | solution.py:205
  29.2 5.6 %collective-permute-start.6 = (bf16[2,752,384]{2,1,0:T(8,128)(2,1)S(1)}, bf16[2,752,384]{2,1,0:T(8,128)(2,1)}, u32[]{:S(2)}, u32[]{:S(2)}) collective-permute-start(bf16[2,752,384]{2,1,0:T(8,128)(2,1)S(1)} %get-tuple-element.32.refs_1_), channel_id=1, source_target_pairs={{0,4},{4,8},{8,12},{1,5},{5,9},{9,13},{2,6},{6,10},{10,14},{3,7},{... | collective-permute-start | bytes 3465224 | tf_op jit(solution)/shard_map/ppermute | solution.py:188
  36.6 1.4 copy.44
  38.0 2.5 %reshape.75.refs_3_ = bf16[2,288,240]{2,1,0:T(8,128)(2,1)} reshape(bf16[2,9,32,5,48]{4,3,2,1,0:T(8,128)(2,1)} %copy.44) | data formatting | bytes 552960 | tf_op jit(solution)/shard_map/reshape | solution.py:205
  41.1 1.4 copy.53
  42.5 2.5 %reshape.77.refs_3_ = bf16[2,288,240]{2,1,0:T(8,128)(2,1)} reshape(bf16[2,9,32,5,48]{4,3,2,1,0:T(8,128)(2,1)} %copy.53) | data formatting | bytes 552960 | tf_op jit(solution)/shard_map/reshape | solution.py:205
  45.1 2.5 %collective-permute-done.3.refs_2_ = bf16[2,752,384]{2,1,0:T(8,128)(2,1)} collective-permute-done((bf16[2,752,384]{2,1,0:T(8,128)(2,1)S(1)}, bf16[2,752,384]{2,1,0:T(8,128)(2,1)}, u32[]{:S(2)}, u32[]{:S(2)}) %collective-permute-start.3) | collective-permute-done | bytes 1155104 | tf_op jit(solution)/shard_map/ppermute | solution.py:189
  49.5 14.7 %shard_map.111 = (bf16[2,752,384]{2,1,0:T(8,128)(2,1)S(1)}, f32[2,736,384]{2,1,0:T(8,128)}) custom-call(bf16[2,752,384]{2,1,0:T(8,128)(2,1)} %collective-permute-done.2.refs_0_, bf16[2,752,384]{2,1,0:T(8,128)(2,1)S(1)} %get-tuple-element.33.refs_1_, bf16[2,752,384]{2,1,0:T(8,128)(2,1)} %collective-permute-done.3.refs_2_, bf16[2,288,240]{2,1,0:T(8,128)(2,1)S(1)} %copy-done.1, ...), custom_call_target="tpu_custom_call" | custom-call | flops 6945767424 | bytes 10485760 | tf_op jit(solution)/shard_map/pallas_call | solution.py:175
  64.2 2.6 %collective-permute-start.4 = (bf16[2,752,384]{2,1,0:T(8,128)(2,1)S(1)}, bf16[2,752,384]{2,1,0:T(8,128)(2,1)S(1)}, u32[]{:S(2)}, u32[]{:S(2)}) collective-permute-start(bf16[2,752,384]{2,1,0:T(8,128)(2,1)S(1)} %get-tuple-element.8.refs_1_), channel_id=1, source_target_pairs={{0,4},{4,8},{8,12},{1,5},{5,9},{9,13},{2,6},{6,10},{10,14},{3,7},{... | collective-permute-start | bytes 3465224 | tf_op jit(solution)/shard_map/ppermute | solution.py:188
  66.8 1.5 collective-permute-start.5
  68.3 3.4 %collective-permute-done.7.refs_2_ = bf16[2,752,384]{2,1,0:T(8,128)(2,1)} collective-permute-done((bf16[2,752,384]{2,1,0:T(8,128)(2,1)S(1)}, bf16[2,752,384]{2,1,0:T(8,128)(2,1)}, u32[]{:S(2)}, u32[]{:S(2)}) %collective-permute-start.7) | collective-permute-done | bytes 1155104 | tf_op jit(solution)/shard_map/ppermute | solution.py:189
  71.7 15.2 %shard_map.113.refs_1_.refs_4_ = bf16[2,752,384]{2,1,0:T(8,128)(2,1)S(1)} custom-call(bf16[2,752,384]{2,1,0:T(8,128)(2,1)} %collective-permute-done.6.refs_0_, bf16[2,752,384]{2,1,0:T(8,128)(2,1)S(1)} %get-tuple-element.32.refs_1_, bf16[2,752,384]{2,1,0:T(8,128)(2,1)} %collective-permute-done.7.refs_2_, bf16[2,288,240]{2,1,0:T(8,128)(2,1)S(1)} %copy-done.5, ...), custom_call_target="tpu_custom_call" | custom-call | flops 6945767424 | bytes 10485760 | tf_op jit(solution)/shard_map/pallas_call | solution.py:175
  86.9 1.8 collective-permute-start.8
  90.0 15.7 %shard_map.115 = f32[432,384]{1,0:T(8,128)S(1)} custom-call(bf16[2,752,384]{2,1,0:T(8,128)(2,1)} %collective-permute-done.2.refs_0_, bf16[2,752,384]{2,1,0:T(8,128)(2,1)S(1)} %get-tuple-element.33.refs_1_, bf16[2,752,384]{2,1,0:T(8,128)(2,1)} %collective-permute-done.3.refs_2_, bf16[2,288,240]{2,1,0:T(8,128)(2,1)S(1)} %copy-done.2, ...), custom_call_target="tpu_custom_call" | custom-call | flops 6945767424 | bytes 10485760 | tf_op jit(solution)/shard_map/pallas_call | solution.py:175
  106.7 18.5 %shard_map.112 = (bf16[2,720,384]{2,1,0:T(8,128)(2,1)}, f32[432,384]{1,0:T(8,128)S(1)}) custom-call(bf16[2,752,384]{2,1,0:T(8,128)(2,1)S(1)} %collective-permute-done.4.refs_0_, bf16[2,752,384]{2,1,0:T(8,128)(2,1)S(1)} %get-tuple-element.8.refs_1_, bf16[2,752,384]{2,1,0:T(8,128)(2,1)S(1)} %collective-permute-done.5.refs_2_, ...), custom_call_target="tpu_custom_call" | custom-call | flops 10418651136 | bytes 10485760 | tf_op jit(solution)/shard_map/pallas_call | solution.py:175
  125.5 40.9 %shard_map.116 = f32[896,384]{1,0:T(8,128)S(1)} custom-call(f32[896,384]{1,0:T(8,128)S(1)} %maximum_maximum_fusion.part), custom_call_target="tpu_custom_call" | custom-call | bytes 20971520 | tf_op jit(solution)/shard_map/pallas_call | solution.py:313
  167.6 13.8 %shard_map.114 = bf16[2,720,384]{2,1,0:T(8,128)(2,1)} custom-call(bf16[2,752,384]{2,1,0:T(8,128)(2,1)S(1)} %collective-permute-done.8.refs_0_, bf16[2,752,384]{2,1,0:T(8,128)(2,1)S(1)} %shard_map.113.refs_1_.refs_4_, bf16[2,752,384]{2,1,0:T(8,128)(2,1)S(1)} %collective-permute-done.9.refs_2_, bf16[2,288,240]{2,1,0:T(8,128)(2,1)S(1)} %copy-done.3, ...), custom_call_target="tpu_custom_call" | custom-call | flops 6945767424 | bytes 10485760 | tf_op jit(solution)/shard_map/pallas_call | solution.py:175
  (82 shorter events, 17.6 us)
Async XLA Ops:
  1.4 10.3 %collective-permute-start = (bf16[2,2,8,384]{3,2,1,0:T(8,128)(2,1)S(1)}, bf16[2,2,8,384]{3,2,1,0:T(8,128)(2,1)S(1)}, u32[]{:S(2)}, u32[]{:S(2)}) collective-permute-start(bf16[2,2,8,384]{3,2,1,0:T(8,128)(2,1)S(1)} %pad_maximum_fusion), channel_id=1, source_target_pairs={{0,2},{2,0},{1,3},{3,1},{4,6},{6,4},{5,7},{7,5},{8,10},{10,8},{9,1... | collective-permute-start | bytes 73736 | tf_op jit(solution)/shard_map/ppermute | solution.py:341
  4.4 7.3 %collective-permute-start.1 = (bf16[2,2,8,384]{3,2,1,0:T(8,128)(2,1)S(1)}, bf16[2,2,8,384]{3,2,1,0:T(8,128)(2,1)S(1)}, u32[]{:S(2)}, u32[]{:S(2)}) collective-permute-start(bf16[2,2,8,384]{3,2,1,0:T(8,128)(2,1)S(1)} %pad_maximum_fusion.1), channel_id=1, source_target_pairs={{2,0},{0,2},{3,1},{1,3},{6,4},{4,6},{7,5},{5,7},{10,8},{8,10},{11,... | collective-permute-start | bytes 73736 | tf_op jit(solution)/shard_map/ppermute | solution.py:342
  5.5 4.8 %copy-start.11 = (s32[2,3]{1,0:T(2,128)}, s32[2,3]{1,0:T(2,128)S(1)}, u32[]{:S(2)}) copy-start(s32[2,3]{1,0:T(2,128)S(1)} %copy.37) | copy-start | bytes 76
  5.5 4.7 %copy-start.13 = (s32[2,5]{1,0:T(2,128)}, s32[2,5]{1,0:T(2,128)S(1)}, u32[]{:S(2)}) copy-start(s32[2,5]{1,0:T(2,128)S(1)} %iota_add_fusion) | copy-start | bytes 124
  8.0 3.8 %copy-start = (bf16[1,2,720,384]{3,2,1,0:T(8,128)(2,1)S(1)}, bf16[1,2,720,384]{3,2,1,0:T(8,128)(2,1)}, u32[]{:S(2)}) copy-start(bf16[1,2,720,384]{3,2,1,0:T(8,128)(2,1)} %param.9) | copy-start | bytes 3317764
  8.0 3.8 %copy-start.9 = (bf16[1,2,720,384]{3,2,1,0:T(8,128)(2,1)S(1)}, bf16[1,2,720,384]{3,2,1,0:T(8,128)(2,1)}, u32[]{:S(2)}) copy-start(bf16[1,2,720,384]{3,2,1,0:T(8,128)(2,1)} %param.8) | copy-start | bytes 3317764
  12.3 32.8 %collective-permute-start.2 = (bf16[2,752,384]{2,1,0:T(8,128)(2,1)S(1)}, bf16[2,752,384]{2,1,0:T(8,128)(2,1)}, u32[]{:S(2)}, u32[]{:S(2)}) collective-permute-start(bf16[2,752,384]{2,1,0:T(8,128)(2,1)S(1)} %get-tuple-element.33.refs_1_), channel_id=1, source_target_pairs={{0,4},{4,8},{8,12},{1,5},{5,9},{9,13},{2,6},{6,10},{10,14},{3,7},{... | collective-permute-start | bytes 3465224 | tf_op jit(solution)/shard_map/ppermute | solution.py:188
  17.2 30.4 %collective-permute-start.3 = (bf16[2,752,384]{2,1,0:T(8,128)(2,1)S(1)}, bf16[2,752,384]{2,1,0:T(8,128)(2,1)}, u32[]{:S(2)}, u32[]{:S(2)}) collective-permute-start(bf16[2,752,384]{2,1,0:T(8,128)(2,1)S(1)} %get-tuple-element.33.refs_1_), channel_id=1, source_target_pairs={{4,0},{8,4},{12,8},{5,1},{9,5},{13,9},{6,2},{10,6},{14,10},{7,3},{... | collective-permute-start | bytes 3465224 | tf_op jit(solution)/shard_map/ppermute | solution.py:189
  26.5 2.5 %copy-start.12 = (s32[2,3]{1,0:T(2,128)S(1)}, s32[2,3]{1,0:T(2,128)}, u32[]{:S(2)}) copy-start(s32[2,3]{1,0:T(2,128)} %copy-done.11) | copy-start | bytes 76
  26.5 2.5 %copy-start.14 = (s32[2,5]{1,0:T(2,128)S(1)}, s32[2,5]{1,0:T(2,128)}, u32[]{:S(2)}) copy-start(s32[2,5]{1,0:T(2,128)} %copy-done.13) | copy-start | bytes 124
  29.2 39.0 %collective-permute-start.6 = (bf16[2,752,384]{2,1,0:T(8,128)(2,1)S(1)}, bf16[2,752,384]{2,1,0:T(8,128)(2,1)}, u32[]{:S(2)}, u32[]{:S(2)}) collective-permute-start(bf16[2,752,384]{2,1,0:T(8,128)(2,1)S(1)} %get-tuple-element.32.refs_1_), channel_id=1, source_target_pairs={{0,4},{4,8},{8,12},{1,5},{5,9},{9,13},{2,6},{6,10},{10,14},{3,7},{... | collective-permute-start | bytes 3465224 | tf_op jit(solution)/shard_map/ppermute | solution.py:188
  34.8 36.9 %collective-permute-start.7 = (bf16[2,752,384]{2,1,0:T(8,128)(2,1)S(1)}, bf16[2,752,384]{2,1,0:T(8,128)(2,1)}, u32[]{:S(2)}, u32[]{:S(2)}) collective-permute-start(bf16[2,752,384]{2,1,0:T(8,128)(2,1)S(1)} %get-tuple-element.32.refs_1_), channel_id=1, source_target_pairs={{4,0},{8,4},{12,8},{5,1},{9,5},{13,9},{6,2},{10,6},{14,10},{7,3},{... | collective-permute-start | bytes 3465224 | tf_op jit(solution)/shard_map/ppermute | solution.py:189
  38.0 2.5 %copy-start.10 = (bf16[2,5,9,9]{3,2,1,0:T(8,128)(2,1)S(1)}, bf16[2,5,9,9]{3,2,1,0:T(8,128)(2,1)}, u32[]{:S(2)}) copy-start(bf16[2,5,9,9]{3,2,1,0:T(8,128)(2,1)} %get-tuple-element.12) | copy-start | bytes 4864
  48.5 1.0 copy-start.7
  49.5 22.2 %copy-start.5 = (bf16[2,288,240]{2,1,0:T(8,128)(2,1)S(1)}, bf16[2,288,240]{2,1,0:T(8,128)(2,1)}, u32[]{:S(2)}) copy-start(bf16[2,288,240]{2,1,0:T(8,128)(2,1)} %reshape.76.refs_3_) | copy-start | bytes 829444
  49.5 22.2 %copy-start.6 = (bf16[432,384]{1,0:T(8,128)(2,1)S(1)}, bf16[432,384]{1,0:T(8,128)(2,1)}, u32[]{:S(2)}) copy-start(bf16[432,384]{1,0:T(8,128)(2,1)} %refs_4_.6) | copy-start | bytes 995332
  64.2 41.6 %collective-permute-start.4 = (bf16[2,752,384]{2,1,0:T(8,128)(2,1)S(1)}, bf16[2,752,384]{2,1,0:T(8,128)(2,1)S(1)}, u32[]{:S(2)}, u32[]{:S(2)}) collective-permute-start(bf16[2,752,384]{2,1,0:T(8,128)(2,1)S(1)} %get-tuple-element.8.refs_1_), channel_id=1, source_target_pairs={{0,4},{4,8},{8,12},{1,5},{5,9},{9,13},{2,6},{6,10},{10,14},{3,7},{... | collective-permute-start | bytes 3465224 | tf_op jit(solution)/shard_map/ppermute | solution.py:188
  66.8 39.1 %collective-permute-start.5 = (bf16[2,752,384]{2,1,0:T(8,128)(2,1)S(1)}, bf16[2,752,384]{2,1,0:T(8,128)(2,1)S(1)}, u32[]{:S(2)}, u32[]{:S(2)}) collective-permute-start(bf16[2,752,384]{2,1,0:T(8,128)(2,1)S(1)} %get-tuple-element.8.refs_1_), channel_id=1, source_target_pairs={{4,0},{8,4},{12,8},{5,1},{9,5},{13,9},{6,2},{10,6},{14,10},{7,3},{... | collective-permute-start | bytes 3465224 | tf_op jit(solution)/shard_map/ppermute | solution.py:189
  71.7 18.3 %copy-start.2 = (bf16[2,288,240]{2,1,0:T(8,128)(2,1)S(1)}, bf16[2,288,240]{2,1,0:T(8,128)(2,1)}, u32[]{:S(2)}) copy-start(bf16[2,288,240]{2,1,0:T(8,128)(2,1)} %reshape.74.refs_3_) | copy-start | bytes 829444
  86.9 80.7 %collective-permute-start.8 = (bf16[2,752,384]{2,1,0:T(8,128)(2,1)S(1)}, bf16[2,752,384]{2,1,0:T(8,128)(2,1)S(1)}, u32[]{:S(2)}, u32[]{:S(2)}) collective-permute-start(bf16[2,752,384]{2,1,0:T(8,128)(2,1)S(1)} %shard_map.113.refs_1_.refs_4_), channel_id=1, source_target_pairs={{0,4},{4,8},{8,12},{1,5},{5,9},{9,13},{2,6},{6,10},{10,14},{3,7},{... | collective-permute-start | bytes 3465224 | tf_op jit(solution)/shard_map/ppermute | solution.py:188
  88.7 78.9 %collective-permute-start.9 = (bf16[2,752,384]{2,1,0:T(8,128)(2,1)S(1)}, bf16[2,752,384]{2,1,0:T(8,128)(2,1)S(1)}, u32[]{:S(2)}, u32[]{:S(2)}) collective-permute-start(bf16[2,752,384]{2,1,0:T(8,128)(2,1)S(1)} %shard_map.113.refs_1_.refs_4_), channel_id=1, source_target_pairs={{4,0},{8,4},{12,8},{5,1},{9,5},{13,9},{6,2},{10,6},{14,10},{7,3},{... | collective-permute-start | bytes 3465224 | tf_op jit(solution)/shard_map/ppermute | solution.py:189
  105.8 1.0 copy-start.4
  166.4 1.2 copy-start.3
  166.4 1.2 copy-start.8
  (1 other events, 1.0 us)

commit v2 on v1

--- a/solution.py
+++ b/solution.py
@@ -2,6 +2,7 @@
 
 import jax
 import jax.numpy as jnp
+import numpy as np
 from jax import lax
 from jax.experimental import pallas as pl
 from jax.experimental.pallas import tpu as pltpu
@@ -32,8 +33,10 @@
     return jnp.concatenate([wide, gap], axis=0), jnp.concatenate([gap, rest], axis=0)
 
 
-def layer_kernel(mode, width, cols, turn, valid, with_mix, with_grad, *refs):
+def layer_kernel(mode, width, cols, turn, valid, with_mix, with_grad, sharing, *refs):
     refs = list(refs)
+    if sharing:
+        refs, shared = refs[: -sharing[-1]], refs[-sharing[-1] :]
     up, own, down, band = refs[:4]
     refs = refs[4:]
     if with_mix:
@@ -44,6 +47,10 @@
         grad_in = refs.pop(0)
         turned = refs.pop()
         padded = refs.pop()
+    phases = iter(())
+    if sharing:
+        parts = [refs.pop(0), refs.pop(0)]
+        phases = sum_phases(*sharing[:-1], parts, refs.pop(1), *shared)
     if with_mix:
         weights = refs[-2:]
         refs = refs[:-2]
@@ -51,6 +58,7 @@
     refs = refs[:-2]
     rows = [up.at[0], up.at[1], own.at[0], own.at[1], down.at[0], down.at[1]]
 
+    next(phases, None)
     if with_mix:
         cg = mix_ref.shape[1] // G
 
@@ -77,7 +85,11 @@
                 highs[pl.ds(at, TILE), k * HALF : (k + 1) * HALF] = piece[:, 128:]
         return carry
 
-    lax.fori_loop(0, width // TILE, basis, 0)
+    blocks = width // TILE
+    lax.fori_loop(0, blocks // 2, basis, 0)
+    next(phases, None)
+    lax.fori_loop(blocks // 2, blocks, basis, 0)
+    next(phases, None)
 
     if with_mix:
         step = width // 2
@@ -104,7 +116,11 @@
                 refs[0][r, width : width + MARGIN, :] = jnp.zeros((MARGIN, total.shape[1]), BF16)
             return carry
 
-        lax.fori_loop(0, ROWS, mix, 0)
+        for r in range(ROWS):
+            lax.fori_loop(r, r + 1, mix, 0)
+            next(phases, None)
+        for _ in phases:
+            pass
 
     if with_grad:
         out = refs[-1]
@@ -146,7 +162,7 @@
         lax.fori_loop(0, K, grad, 0)
 
 
-def layer(mode, cols, halo, band, weights=None, turn=False, slope=None, grad=None, valid=None):
+def layer(mode, cols, halo, band, weights=None, turn=False, slope=None, grad=None, valid=None, parts=None, scale=None):
     chan = halo[1].shape[2]
     width = halo[1].shape[1] - MARGIN
     with_mix, with_grad = weights is not None, grad is not None
@@ -160,6 +176,12 @@
         outs.append(jax.ShapeDtypeStruct((ROWS, width, chan), F32))
     if mode == "scale":
         args.append(slope)
+    sharing, shared, extra = None, [], {}
+    if parts is not None:
+        args += parts
+        sharing, shared, outs_more = sum_plan(parts, scale)
+        outs.append(outs_more)
+        extra = dict(collective_id=0, has_side_effects=True)
     depth = ROWS * width
     if with_grad:
         args.append(grad)
@@ -173,12 +195,12 @@
     vmem = pl.BlockSpec(memory_space=pltpu.VMEM)
     flops = 2 * ROWS * width * K * HALF * 2 * HALF * (1 + with_mix + with_grad)
     return pl.pallas_call(
-        functools.partial(layer_kernel, mode, width, cols, turn, valid, with_mix, with_grad),
+        functools.partial(layer_kernel, mode, width, cols, turn, valid, with_mix, with_grad, sharing),
         out_shape=tuple(outs),
         in_specs=[vmem] * len(args),
         out_specs=tuple([vmem] * len(outs)),
-        scratch_shapes=scratch,
-        compiler_params=pltpu.CompilerParams(vmem_limit_bytes=48 * 2**20),
+        scratch_shapes=scratch + shared,
+        compiler_params=pltpu.CompilerParams(vmem_limit_bytes=48 * 2**20, **extra),
         cost_estimate=pl.CostEstimate(flops=flops, bytes_accessed=10 * 2**20, transcendentals=0),
     )(*args)
 
@@ -221,7 +243,24 @@
     return banded(pull.astype(BF16)), banded(jnp.flip(push, 3).astype(BF16))
 
 
-def sum_kernel(axes, sizes, total, part, result, *scratch):
+def sum_plan(parts, scale):
+    axes = ("ens", "lon", "lat")
+    sizes = [lax.axis_size(axis) for axis in axes]
+    rows = sum(part.shape[0] for part in parts)
+    chan = parts[0].shape[1]
+    devices = sizes[0] * sizes[1] * sizes[2]
+    total = -(-rows // (16 * devices)) * 16 * devices
+    slots, extent, count = [], total, 0
+    for size in sizes:
+        extent //= size
+        slots.append(pltpu.VMEM((size - 1, extent, chan), BF16))
+        count += 2 * (size - 1)
+    scratch = [pltpu.VMEM((total, chan), F32), pltpu.VMEM((total, chan), BF16)] + slots
+    scratch += [pltpu.SemaphoreType.DMA((count,)), pltpu.SemaphoreType.DMA((count,))]
+    return (axes, sizes, total, scale, len(scratch)), scratch, jax.ShapeDtypeStruct((total, chan), BF16)
+
+
+def sum_phases(axes, sizes, total, scale, parts, result, held, wire, *scratch):
     slots = scratch[: len(axes)]
     send_sem, recv_sem = scratch[len(axes) :]
     places = [lax.axis_index(axis) for axis in axes]
@@ -232,6 +271,12 @@
             peer = lax.rem(place + d, size)
             pl.semaphore_signal(barrier, inc=1, device_id={axis: peer}, device_id_type=pl.DeviceIdType.MESH)
             greeted += 1
+    at = 0
+    for part in parts:
+        held[at : at + part.shape[0], :] = part[...] * scale
+        at += part.shape[0]
+    held[at:, :] = jnp.zeros((total - at, held.shape[1]), F32)
+    wire[...] = held[...].astype(BF16)
     pl.semaphore_wait(barrier, greeted)
 
     used = 0
@@ -239,7 +284,7 @@
     bases = []
 
     def block(ref, start, count):
-        return ref.at[pl.ds(pl.multiple_of(start, 8), count)]
+        return ref.at[pl.ds(pl.multiple_of(start, 16), count)]
 
     for level, (axis, size, place) in enumerate(zip(axes, sizes, places)):
         bases.append((base, extent))
@@ -248,7 +293,7 @@
         for d in range(1, size):
             peer = lax.rem(place + d, size)
             copy = pltpu.make_async_remote_copy(
-                src_ref=block(part, base + peer * extent, extent),
+                src_ref=block(wire, base + peer * extent, extent),
                 dst_ref=slots[level].at[d - 1],
                 send_sem=send_sem.at[used],
                 recv_sem=recv_sem.at[used],
@@ -259,22 +304,25 @@
             copies.append(copy)
             used += 1
         base = base + place * extent
+        yield
         for copy in copies:
             copy.wait()
-        mine = pl.ds(pl.multiple_of(base, 8), extent)
-        value = part[mine, :]
+        mine = pl.ds(pl.multiple_of(base, 16), extent)
+        value = held[mine, :]
         for d in range(1, size):
-            value = value + slots[level][d - 1]
-        part[mine, :] = value
-    result[mine, :] = value
+            value = value + slots[level][d - 1].astype(F32)
+        if level < len(axes) - 1:
+            held[mine, :] = value
+            wire[mine, :] = value.astype(BF16)
+    result[mine, :] = value.astype(BF16)
     for level in reversed(range(len(axes))):
         axis, size, place = axes[level], sizes[level], places[level]
         outer, whole = bases[level]
         extent = whole // size
+        own = outer + place * extent
         copies = []
         for d in range(1, size):
             peer = lax.rem(place + d, size)
-            own = outer + place * extent
             copy = pltpu.make_async_remote_copy(
                 src_ref=block(result, own, extent),
                 dst_ref=block(result, own, extent),
@@ -286,43 +334,9 @@
             copy.start()
             copies.append(copy)
             used += 1
+        yield
         for copy in copies:
             copy.wait()
-
-
-def summed(parts, scale):
-    axes = ("ens", "lon", "lat")
-    sizes = [lax.axis_size(axis) for axis in axes]
-    rows = sum(part.shape[0] for part in parts)
-    chan = parts[0].shape[1]
-    devices = sizes[0] * sizes[1] * sizes[2]
-    total = -(-rows // (8 * devices)) * 8 * devices
-    filler = jnp.zeros((total - rows, chan), F32)
-    stacked = jnp.concatenate([part * scale for part in parts] + [filler], axis=0)
-    slots, extent, count = [], total, 0
-    for size in sizes:
-        extent //= size
-        slots.append(pltpu.VMEM((size - 1, extent, chan), F32))
-        count += 2 * (size - 1)
-
-    def kernel(part, result, held, *scratch):
-        held[...] = part[...]
-        sum_kernel(axes, sizes, total, held, result, *scratch)
-
-    vmem = pl.BlockSpec(memory_space=pltpu.VMEM)
-    return pl.pallas_call(
-        kernel,
-        out_shape=jax.ShapeDtypeStruct((total, chan), F32),
-        in_specs=[vmem],
-        out_specs=vmem,
-        scratch_shapes=[pltpu.VMEM((total, chan), F32)]
-        + slots
-        + [pltpu.SemaphoreType.DMA((count,)), pltpu.SemaphoreType.DMA((count,))],
-        compiler_params=pltpu.CompilerParams(
-            collective_id=0, has_side_effects=True, vmem_limit_bytes=32 * 2**20
-        ),
-        cost_estimate=pl.CostEstimate(flops=0, bytes_accessed=20 * 2**20, transcendentals=0),
-    )(stacked)
 
 
 def shards(fields, cotangent, filter_one, filter_two, mix_one, mix_two, source_rows, band_width):
@@ -359,10 +373,11 @@
     inner = (WHALF, WHALF + cols)
     (part_one,) = layer("none", cols, fields_halo, pull_one, grad=pre_grad, valid=inner)
     forward, part_two = layer("plain", cols, hidden_halo, pull_two, mix_two, grad=cot, valid=(0, cols))
-    (adjoint,) = layer("plain", cols, pre_halo, push_one, mix_one, turn=True)
-
-    factor = 1.0 / jnp.sqrt(jnp.float32(total_rows * total_cols * lax.axis_size("ens")))
-    sums = summed([part_one, part_two], factor)
+    factor = float(1.0 / np.sqrt(np.float32(total_rows * total_cols * lax.axis_size("ens"))))
+    adjoint, sums = layer(
+        "plain", cols, pre_halo, push_one, mix_one, turn=True, parts=[part_one, part_two], scale=factor
+    )
+    sums = sums.astype(F32)
     length = part_one.shape[0]
     total_one, total_two = sums[:length], sums[length : 2 * length]
     return forward[None], adjoint[None], total_one, total_two

time: 183 us -> 159 us (0.87)
  Pallas kernels: 119 us -> 94.2 us
    pallas_call x1 -> x0, Pallas kernels: 40.9 us -> none  [summed(): pl.pallas_call(kernel, out_shape=jax.ShapeDtypeStruct((total, chan), F32)...]
    pallas_call x5, Pallas kernels: 77.9 us -> 94.2 us  [layer(): pl.pallas_call(functools.partial(layer_kernel, mode, width, cols, turn, v...]
    unnamed x31 -> x34, local copies, waits for them, and re-layouts: 3.66 us -> 4.76 us
  transfers between devices with their start and end apart: 10 -> 10, of which waited for: 2 -> 2; matrix products, arithmetic and copies ran while one was open for 16% -> 17% of each run, Pallas kernels for 58% -> 40%
where the time goes in v2:
time: 159 us; the launch traced here: 158 us
  Pallas kernels  94.2 us (59%)
  local copies, waits for them, and re-layouts  25.5 us (16%)
  starting transfers between devices  23.4 us (15%)
  waiting for transfers between devices  6.61 us (4%)
  other arithmetic  4.95 us (3%)
  matrix products  2.49 us (2%)
    pallas_call x5, Pallas kernels, layer(): pl.pallas_call(functools.partial(layer_kernel, mode, width, cols, turn, v...  94.2 us
    ppermute x4, starting transfers between devices, exchanged(): up = lax.ppermute(block, 'lat', [(i, i + 1) for i in range(count - 1)])  15.2 us
    reshape x4, local copies, waits for them, and re-layouts, banded(): return out.astype(BF16).reshape(ROWS, K * TILE, NEAR * SPAN)  9.91 us
    ppermute x4, waiting for transfers between devices, exchanged(): down = lax.ppermute(block, 'lat', [(i + 1, i) for i in range(count - 1)])  6.6 us
    convert_element_type x4, local copies, waits for them, and re-layouts, banded(): return out.astype(BF16).reshape(ROWS, K * TILE, NEAR * SPAN)  5.39 us
    ppermute x4, starting transfers between devices, exchanged(): down = lax.ppermute(block, 'lat', [(i + 1, i) for i in range(count - 1)])  5.14 us
    unnamed x34, local copies, waits for them, and re-layouts  4.76 us
  transfers between devices with their start and end apart: 10, of which 2 were waited for; matrix products, arithmetic and copies ran while one was open for 17% of the time, Pallas kernels for 40%

profile of v2, /device:TPU:0, one launch (start us, length us, event | category | flops | bytes accessed | tf_op | source)
XLA Modules:
  0.0 158.1 jit_solution(16770511266069578914)
XLA Ops:
  1.4 3.0 %collective-permute-start = (bf16[2,2,8,384]{3,2,1,0:T(8,128)(2,1)S(1)}, bf16[2,2,8,384]{3,2,1,0:T(8,128)(2,1)S(1)}, u32[]{:S(2)}, u32[]{:S(2)}) collective-permute-start(bf16[2,2,8,384]{3,2,1,0:T(8,128)(2,1)S(1)} %pad_maximum_fusion), channel_id=1, source_target_pairs={{0,2},{2,0},{1,3},{3,1},{4,6},{6,4},{5,7},{7,5},{8,10},{10,8},{9,1... | collective-permute-start | bytes 73736 | tf_op jit(solution)/shard_map/ppermute | solution.py:355
  10.2 1.3 fusion.33
  12.2 4.9 %collective-permute-start.2 = (bf16[2,752,384]{2,1,0:T(8,128)(2,1)S(1)}, bf16[2,752,384]{2,1,0:T(8,128)(2,1)}, u32[]{:S(2)}, u32[]{:S(2)}) collective-permute-start(bf16[2,752,384]{2,1,0:T(8,128)(2,1)S(1)} %get-tuple-element.37.refs_1_), channel_id=1, source_target_pairs={{0,4},{4,8},{8,12},{1,5},{5,9},{9,13},{2,6},{6,10},{10,14},{3,7},{... | collective-permute-start | bytes 3465224 | tf_op jit(solution)/shard_map/ppermute | solution.py:210
  18.4 1.3 copy.41
  19.7 2.5 %reshape.74.refs_3_ = bf16[2,288,240]{2,1,0:T(8,128)(2,1)} reshape(bf16[2,9,32,5,48]{4,3,2,1,0:T(8,128)(2,1)} %copy.41) | data formatting | bytes 552960 | tf_op jit(solution)/shard_map/reshape | solution.py:227
  22.3 2.0 %fusion.10 = (bf16[2,5,9,9]{3,2,1,0:T(8,128)(2,1)}, bf16[2,5,9,9]{3,2,1,0:T(8,128)(2,1)S(1)}) fusion(f32[1,5,3,9,9]{4,2,3,1,0:T(4,128)} %get-tuple-element.27, f32[1,5,3,9,9]{4,2,3,1,0:T(4,128)} %get-tuple-element.26, pred[2,5,3]{2,1,0:T(8,128)(4,1)S(1)} %copy.45, f32[1,5,3,9,9]{4,2,3,1,0:T(4,128)} %get-tuple-element.25, f32[1,5,3,9,9]{4,2,3,1,0:T(4,128)} %get-tuple-element.24), kind=kLoop, calls=%fused_computation.17 | loop fusion | flops 12960 | bytes 22710 | tf_op jit(solution)/shard_map/reduce_sum | solution.py:242
  25.0 1.3 copy.49
  26.3 2.5 %reshape.76.refs_3_ = bf16[2,288,240]{2,1,0:T(8,128)(2,1)} reshape(bf16[2,9,32,5,48]{4,3,2,1,0:T(8,128)(2,1)} %copy.49) | data formatting | bytes 552960 | tf_op jit(solution)/shard_map/reshape | solution.py:227
  29.1 5.6 %collective-permute-start.6 = (bf16[2,752,384]{2,1,0:T(8,128)(2,1)S(1)}, bf16[2,752,384]{2,1,0:T(8,128)(2,1)}, u32[]{:S(2)}, u32[]{:S(2)}) collective-permute-start(bf16[2,752,384]{2,1,0:T(8,128)(2,1)S(1)} %get-tuple-element.36.refs_1_), channel_id=1, source_target_pairs={{0,4},{4,8},{8,12},{1,5},{5,9},{9,13},{2,6},{6,10},{10,14},{3,7},{... | collective-permute-start | bytes 3465224 | tf_op jit(solution)/shard_map/ppermute | solution.py:210
  36.5 1.3 copy.44
  37.8 2.5 %reshape.75.refs_3_ = bf16[2,288,240]{2,1,0:T(8,128)(2,1)} reshape(bf16[2,9,32,5,48]{4,3,2,1,0:T(8,128)(2,1)} %copy.44) | data formatting | bytes 552960 | tf_op jit(solution)/shard_map/reshape | solution.py:227
  41.0 1.3 copy.53
  42.3 2.5 %reshape.77.refs_3_ = bf16[2,288,240]{2,1,0:T(8,128)(2,1)} reshape(bf16[2,9,32,5,48]{4,3,2,1,0:T(8,128)(2,1)} %copy.53) | data formatting | bytes 552960 | tf_op jit(solution)/shard_map/reshape | solution.py:227
  44.8 2.6 %collective-permute-done.3.refs_2_ = bf16[2,752,384]{2,1,0:T(8,128)(2,1)} collective-permute-done((bf16[2,752,384]{2,1,0:T(8,128)(2,1)S(1)}, bf16[2,752,384]{2,1,0:T(8,128)(2,1)}, u32[]{:S(2)}, u32[]{:S(2)}) %collective-permute-start.3) | collective-permute-done | bytes 1155104 | tf_op jit(solution)/shard_map/ppermute | solution.py:211
  49.4 14.4 %shard_map.111 = (bf16[2,752,384]{2,1,0:T(8,128)(2,1)S(1)}, f32[2,736,384]{2,1,0:T(8,128)}) custom-call(bf16[2,752,384]{2,1,0:T(8,128)(2,1)} %collective-permute-done.2.refs_0_, bf16[2,752,384]{2,1,0:T(8,128)(2,1)S(1)} %get-tuple-element.37.refs_1_, bf16[2,752,384]{2,1,0:T(8,128)(2,1)} %collective-permute-done.3.refs_2_, bf16[2,288,240]{2,1,0:T(8,128)(2,1)S(1)} %copy-done.1, ...), custom_call_target="tpu_custom_call" | custom-call | flops 6945767424 | bytes 10485760 | tf_op jit(solution)/shard_map/pallas_call | solution.py:197
  63.8 2.7 %collective-permute-start.4 = (bf16[2,752,384]{2,1,0:T(8,128)(2,1)S(1)}, bf16[2,752,384]{2,1,0:T(8,128)(2,1)S(1)}, u32[]{:S(2)}, u32[]{:S(2)}) collective-permute-start(bf16[2,752,384]{2,1,0:T(8,128)(2,1)S(1)} %get-tuple-element.10.refs_1_), channel_id=1, source_target_pairs={{0,4},{4,8},{8,12},{1,5},{5,9},{9,13},{2,6},{6,10},{10,14},{3,7},{... | collective-permute-start | bytes 3465224 | tf_op jit(solution)/shard_map/ppermute | solution.py:210
  66.6 1.3 collective-permute-start.5
  67.9 3.9 %collective-permute-done.7.refs_2_ = bf16[2,752,384]{2,1,0:T(8,128)(2,1)} collective-permute-done((bf16[2,752,384]{2,1,0:T(8,128)(2,1)S(1)}, bf16[2,752,384]{2,1,0:T(8,128)(2,1)}, u32[]{:S(2)}, u32[]{:S(2)}) %collective-permute-start.7) | collective-permute-done | bytes 1155104 | tf_op jit(solution)/shard_map/ppermute | solution.py:211
  71.8 15.0 %shard_map.113.refs_4_.refs_1_ = bf16[2,752,384]{2,1,0:T(8,128)(2,1)S(1)} custom-call(bf16[2,752,384]{2,1,0:T(8,128)(2,1)} %collective-permute-done.6.refs_0_, bf16[2,752,384]{2,1,0:T(8,128)(2,1)S(1)} %get-tuple-element.36.refs_1_, bf16[2,752,384]{2,1,0:T(8,128)(2,1)} %collective-permute-done.7.refs_2_, bf16[2,288,240]{2,1,0:T(8,128)(2,1)S(1)} %copy-done.5, ...), custom_call_target="tpu_custom_call" | custom-call | flops 6945767424 | bytes 10485760 | tf_op jit(solution)/shard_map/pallas_call | solution.py:197
  86.8 1.9 %collective-permute-start.8 = (bf16[2,752,384]{2,1,0:T(8,128)(2,1)S(1)}, bf16[2,752,384]{2,1,0:T(8,128)(2,1)S(1)}, u32[]{:S(2)}, u32[]{:S(2)}) collective-permute-start(bf16[2,752,384]{2,1,0:T(8,128)(2,1)S(1)} %shard_map.113.refs_4_.refs_1_), channel_id=1, source_target_pairs={{0,4},{4,8},{8,12},{1,5},{5,9},{9,13},{2,6},{6,10},{10,14},{3,7},{... | collective-permute-start | bytes 3465224 | tf_op jit(solution)/shard_map/ppermute | solution.py:210
  88.8 1.3 collective-permute-start.9
  90.1 15.8 %shard_map.114.refs_5_ = f32[432,384]{1,0:T(8,128)S(1)} custom-call(bf16[2,752,384]{2,1,0:T(8,128)(2,1)} %collective-permute-done.2.refs_0_, bf16[2,752,384]{2,1,0:T(8,128)(2,1)S(1)} %get-tuple-element.37.refs_1_, bf16[2,752,384]{2,1,0:T(8,128)(2,1)} %collective-permute-done.3.refs_2_, bf16[2,288,240]{2,1,0:T(8,128)(2,1)S(1)} %copy-done.2, ...), custom_call_target="tpu_custom_call" | custom-call | flops 6945767424 | bytes 10485760 | tf_op jit(solution)/shard_map/pallas_call | solution.py:197
  106.0 18.0 %shard_map.112 = (bf16[2,720,384]{2,1,0:T(8,128)(2,1)}, f32[432,384]{1,0:T(8,128)S(1)}) custom-call(bf16[2,752,384]{2,1,0:T(8,128)(2,1)S(1)} %collective-permute-done.4.refs_0_, bf16[2,752,384]{2,1,0:T(8,128)(2,1)S(1)} %get-tuple-element.10.refs_1_, bf16[2,752,384]{2,1,0:T(8,128)(2,1)S(1)} %collective-permute-done.5.refs_2_, ...), custom_call_target="tpu_custom_call" | custom-call | flops 10418651136 | bytes 10485760 | tf_op jit(solution)/shard_map/pallas_call | solution.py:197
  125.0 30.9 %shard_map.115 = (bf16[2,720,384]{2,1,0:T(8,128)(2,1)S(1)}, bf16[1024,384]{1,0:T(8,128)(2,1)S(1)}) custom-call(bf16[2,752,384]{2,1,0:T(8,128)(2,1)S(1)} %collective-permute-done.8.refs_0_, bf16[2,752,384]{2,1,0:T(8,128)(2,1)S(1)} %shard_map.113.refs_4_.refs_1_, bf16[2,752,384]{2,1,0:T(8,128)(2,1)} %copy-done.15, bf16[2,288,240]{2,1,0:T(8,128)(2,1)S(1)} %copy-done.3, ...), custom_call_target="tpu_custom_call" | custom-call | flops 6945767424 | bytes 10485760 | tf_op jit(solution)/shard_map/pallas_call | solution.py:197
  (79 shorter events, 17.0 us)
Async XLA Ops:
  1.4 10.2 %collective-permute-start = (bf16[2,2,8,384]{3,2,1,0:T(8,128)(2,1)S(1)}, bf16[2,2,8,384]{3,2,1,0:T(8,128)(2,1)S(1)}, u32[]{:S(2)}, u32[]{:S(2)}) collective-permute-start(bf16[2,2,8,384]{3,2,1,0:T(8,128)(2,1)S(1)} %pad_maximum_fusion), channel_id=1, source_target_pairs={{0,2},{2,0},{1,3},{3,1},{4,6},{6,4},{5,7},{7,5},{8,10},{10,8},{9,1... | collective-permute-start | bytes 73736 | tf_op jit(solution)/shard_map/ppermute | solution.py:355
  4.4 7.2 %collective-permute-start.1 = (bf16[2,2,8,384]{3,2,1,0:T(8,128)(2,1)S(1)}, bf16[2,2,8,384]{3,2,1,0:T(8,128)(2,1)S(1)}, u32[]{:S(2)}, u32[]{:S(2)}) collective-permute-start(bf16[2,2,8,384]{3,2,1,0:T(8,128)(2,1)S(1)} %pad_maximum_fusion.1), channel_id=1, source_target_pairs={{2,0},{0,2},{3,1},{1,3},{6,4},{4,6},{7,5},{5,7},{10,8},{8,10},{11,... | collective-permute-start | bytes 73736 | tf_op jit(solution)/shard_map/ppermute | solution.py:356
  5.5 4.7 %copy-start.11 = (s32[2,3]{1,0:T(2,128)}, s32[2,3]{1,0:T(2,128)S(1)}, u32[]{:S(2)}) copy-start(s32[2,3]{1,0:T(2,128)S(1)} %copy.37) | copy-start | bytes 76
  5.5 4.7 %copy-start.13 = (s32[2,5]{1,0:T(2,128)}, s32[2,5]{1,0:T(2,128)S(1)}, u32[]{:S(2)}) copy-start(s32[2,5]{1,0:T(2,128)S(1)} %iota_add_fusion) | copy-start | bytes 124
  8.0 3.7 %copy-start = (bf16[1,2,720,384]{3,2,1,0:T(8,128)(2,1)S(1)}, bf16[1,2,720,384]{3,2,1,0:T(8,128)(2,1)}, u32[]{:S(2)}) copy-start(bf16[1,2,720,384]{3,2,1,0:T(8,128)(2,1)} %param.9) | copy-start | bytes 3317764
  8.0 3.7 %copy-start.9 = (bf16[1,2,720,384]{3,2,1,0:T(8,128)(2,1)S(1)}, bf16[1,2,720,384]{3,2,1,0:T(8,128)(2,1)}, u32[]{:S(2)}) copy-start(bf16[1,2,720,384]{3,2,1,0:T(8,128)(2,1)} %param.8) | copy-start | bytes 3317764
  12.2 32.7 %collective-permute-start.2 = (bf16[2,752,384]{2,1,0:T(8,128)(2,1)S(1)}, bf16[2,752,384]{2,1,0:T(8,128)(2,1)}, u32[]{:S(2)}, u32[]{:S(2)}) collective-permute-start(bf16[2,752,384]{2,1,0:T(8,128)(2,1)S(1)} %get-tuple-element.37.refs_1_), channel_id=1, source_target_pairs={{0,4},{4,8},{8,12},{1,5},{5,9},{9,13},{2,6},{6,10},{10,14},{3,7},{... | collective-permute-start | bytes 3465224 | tf_op jit(solution)/shard_map/ppermute | solution.py:210
  17.1 30.4 %collective-permute-start.3 = (bf16[2,752,384]{2,1,0:T(8,128)(2,1)S(1)}, bf16[2,752,384]{2,1,0:T(8,128)(2,1)}, u32[]{:S(2)}, u32[]{:S(2)}) collective-permute-start(bf16[2,752,384]{2,1,0:T(8,128)(2,1)S(1)} %get-tuple-element.37.refs_1_), channel_id=1, source_target_pairs={{4,0},{8,4},{12,8},{5,1},{9,5},{13,9},{6,2},{10,6},{14,10},{7,3},{... | collective-permute-start | bytes 3465224 | tf_op jit(solution)/shard_map/ppermute | solution.py:211
  26.3 2.5 %copy-start.12 = (s32[2,3]{1,0:T(2,128)S(1)}, s32[2,3]{1,0:T(2,128)}, u32[]{:S(2)}) copy-start(s32[2,3]{1,0:T(2,128)} %copy-done.11) | copy-start | bytes 76
  26.3 2.5 %copy-start.14 = (s32[2,5]{1,0:T(2,128)S(1)}, s32[2,5]{1,0:T(2,128)}, u32[]{:S(2)}) copy-start(s32[2,5]{1,0:T(2,128)} %copy-done.13) | copy-start | bytes 124
  29.1 38.8 %collective-permute-start.6 = (bf16[2,752,384]{2,1,0:T(8,128)(2,1)S(1)}, bf16[2,752,384]{2,1,0:T(8,128)(2,1)}, u32[]{:S(2)}, u32[]{:S(2)}) collective-permute-start(bf16[2,752,384]{2,1,0:T(8,128)(2,1)S(1)} %get-tuple-element.36.refs_1_), channel_id=1, source_target_pairs={{0,4},{4,8},{8,12},{1,5},{5,9},{9,13},{2,6},{6,10},{10,14},{3,7},{... | collective-permute-start | bytes 3465224 | tf_op jit(solution)/shard_map/ppermute | solution.py:210
  34.7 37.1 %collective-permute-start.7 = (bf16[2,752,384]{2,1,0:T(8,128)(2,1)S(1)}, bf16[2,752,384]{2,1,0:T(8,128)(2,1)}, u32[]{:S(2)}, u32[]{:S(2)}) collective-permute-start(bf16[2,752,384]{2,1,0:T(8,128)(2,1)S(1)} %get-tuple-element.36.refs_1_), channel_id=1, source_target_pairs={{4,0},{8,4},{12,8},{5,1},{9,5},{13,9},{6,2},{10,6},{14,10},{7,3},{... | collective-permute-start | bytes 3465224 | tf_op jit(solution)/shard_map/ppermute | solution.py:211
  37.8 2.5 %copy-start.10 = (bf16[2,5,9,9]{3,2,1,0:T(8,128)(2,1)S(1)}, bf16[2,5,9,9]{3,2,1,0:T(8,128)(2,1)}, u32[]{:S(2)}) copy-start(bf16[2,5,9,9]{3,2,1,0:T(8,128)(2,1)} %get-tuple-element.16) | copy-start | bytes 4864
  49.4 22.4 %copy-start.5 = (bf16[2,288,240]{2,1,0:T(8,128)(2,1)S(1)}, bf16[2,288,240]{2,1,0:T(8,128)(2,1)}, u32[]{:S(2)}) copy-start(bf16[2,288,240]{2,1,0:T(8,128)(2,1)} %reshape.76.refs_3_) | copy-start | bytes 829444
  49.4 22.4 %copy-start.6 = (bf16[432,384]{1,0:T(8,128)(2,1)S(1)}, bf16[432,384]{1,0:T(8,128)(2,1)}, u32[]{:S(2)}) copy-start(bf16[432,384]{1,0:T(8,128)(2,1)} %refs_4_.6) | copy-start | bytes 995332
  63.8 42.1 %collective-permute-start.4 = (bf16[2,752,384]{2,1,0:T(8,128)(2,1)S(1)}, bf16[2,752,384]{2,1,0:T(8,128)(2,1)S(1)}, u32[]{:S(2)}, u32[]{:S(2)}) collective-permute-start(bf16[2,752,384]{2,1,0:T(8,128)(2,1)S(1)} %get-tuple-element.10.refs_1_), channel_id=1, source_target_pairs={{0,4},{4,8},{8,12},{1,5},{5,9},{9,13},{2,6},{6,10},{10,14},{3,7},{... | collective-permute-start | bytes 3465224 | tf_op jit(solution)/shard_map/ppermute | solution.py:210
  66.6 39.4 %collective-permute-start.5 = (bf16[2,752,384]{2,1,0:T(8,128)(2,1)S(1)}, bf16[2,752,384]{2,1,0:T(8,128)(2,1)S(1)}, u32[]{:S(2)}, u32[]{:S(2)}) collective-permute-start(bf16[2,752,384]{2,1,0:T(8,128)(2,1)S(1)} %get-tuple-element.10.refs_1_), channel_id=1, source_target_pairs={{4,0},{8,4},{12,8},{5,1},{9,5},{13,9},{6,2},{10,6},{14,10},{7,3},{... | collective-permute-start | bytes 3465224 | tf_op jit(solution)/shard_map/ppermute | solution.py:211
  71.8 18.2 %copy-start.2 = (bf16[2,288,240]{2,1,0:T(8,128)(2,1)S(1)}, bf16[2,288,240]{2,1,0:T(8,128)(2,1)}, u32[]{:S(2)}) copy-start(bf16[2,288,240]{2,1,0:T(8,128)(2,1)} %reshape.74.refs_3_) | copy-start | bytes 829444
  86.8 19.1 %copy-start.4 = (bf16[2,288,240]{2,1,0:T(8,128)(2,1)S(1)}, bf16[2,288,240]{2,1,0:T(8,128)(2,1)}, u32[]{:S(2)}) copy-start(bf16[2,288,240]{2,1,0:T(8,128)(2,1)} %reshape.75.refs_3_) | copy-start | bytes 829444
  86.8 37.1 %collective-permute-start.8 = (bf16[2,752,384]{2,1,0:T(8,128)(2,1)S(1)}, bf16[2,752,384]{2,1,0:T(8,128)(2,1)S(1)}, u32[]{:S(2)}, u32[]{:S(2)}) collective-permute-start(bf16[2,752,384]{2,1,0:T(8,128)(2,1)S(1)} %shard_map.113.refs_4_.refs_1_), channel_id=1, source_target_pairs={{0,4},{4,8},{8,12},{1,5},{5,9},{9,13},{2,6},{6,10},{10,14},{3,7},{... | collective-permute-start | bytes 3465224 | tf_op jit(solution)/shard_map/ppermute | solution.py:210
  88.8 35.2 %collective-permute-start.9 = (bf16[2,752,384]{2,1,0:T(8,128)(2,1)S(1)}, bf16[2,752,384]{2,1,0:T(8,128)(2,1)S(1)}, u32[]{:S(2)}, u32[]{:S(2)}) collective-permute-start(bf16[2,752,384]{2,1,0:T(8,128)(2,1)S(1)} %shard_map.113.refs_4_.refs_1_), channel_id=1, source_target_pairs={{4,0},{8,4},{12,8},{5,1},{9,5},{13,9},{6,2},{10,6},{14,10},{7,3},{... | collective-permute-start | bytes 3465224 | tf_op jit(solution)/shard_map/ppermute | solution.py:211
  105.9 19.1 %copy-start.3 = (bf16[2,288,240]{2,1,0:T(8,128)(2,1)S(1)}, bf16[2,288,240]{2,1,0:T(8,128)(2,1)}, u32[]{:S(2)}) copy-start(bf16[2,288,240]{2,1,0:T(8,128)(2,1)} %reshape.77.refs_3_) | copy-start | bytes 829444
  105.9 19.1 %copy-start.8 = (bf16[432,384]{1,0:T(8,128)(2,1)S(1)}, bf16[432,384]{1,0:T(8,128)(2,1)}, u32[]{:S(2)}) copy-start(bf16[432,384]{1,0:T(8,128)(2,1)} %refs_4_.7) | copy-start | bytes 995332
  124.0 1.0 copy-start.15
  (2 other events, 1.9 us)

commit v3 on v2

--- a/solution.py
+++ b/solution.py
@@ -43,14 +43,15 @@
         mix_ref = refs.pop(0)
     if mode == "scale":
         slope_in = refs.pop(0)
+    if sharing:
+        parts = [refs.pop(0) for _ in range(sharing[-2])]
     if with_grad:
         grad_in = refs.pop(0)
         turned = refs.pop()
         padded = refs.pop()
     phases = iter(())
     if sharing:
-        parts = [refs.pop(0), refs.pop(0)]
-        phases = sum_phases(*sharing[:-1], parts, refs.pop(1), *shared)
+        phases = sum_phases(*sharing[:-2], parts, refs.pop(1), *shared)
     if with_mix:
         weights = refs[-2:]
         refs = refs[:-2]
@@ -119,8 +120,6 @@
         for r in range(ROWS):
             lax.fori_loop(r, r + 1, mix, 0)
             next(phases, None)
-        for _ in phases:
-            pass
 
     if with_grad:
         out = refs[-1]
@@ -161,8 +160,11 @@
 
         lax.fori_loop(0, K, grad, 0)
 
-
-def layer(mode, cols, halo, band, weights=None, turn=False, slope=None, grad=None, valid=None, parts=None, scale=None):
+    for _ in phases:
+        pass
+
+
+def layer(mode, cols, halo, band, weights=None, turn=False, slope=None, grad=None, valid=None, parts=None, scale=None, ident=0):
     chan = halo[1].shape[2]
     width = halo[1].shape[1] - MARGIN
     with_mix, with_grad = weights is not None, grad is not None
@@ -181,7 +183,7 @@
         args += parts
         sharing, shared, outs_more = sum_plan(parts, scale)
         outs.append(outs_more)
-        extra = dict(collective_id=0, has_side_effects=True)
+        extra = dict(collective_id=ident, has_side_effects=True)
     depth = ROWS * width
     if with_grad:
         args.append(grad)
@@ -257,7 +259,7 @@
         count += 2 * (size - 1)
     scratch = [pltpu.VMEM((total, chan), F32), pltpu.VMEM((total, chan), BF16)] + slots
     scratch += [pltpu.SemaphoreType.DMA((count,)), pltpu.SemaphoreType.DMA((count,))]
-    return (axes, sizes, total, scale, len(scratch)), scratch, jax.ShapeDtypeStruct((total, chan), BF16)
+    return (axes, sizes, total, scale, len(parts), len(scratch)), scratch, jax.ShapeDtypeStruct((total, chan), BF16)
 
 
 def sum_phases(axes, sizes, total, scale, parts, result, held, wire, *scratch):
@@ -355,31 +357,40 @@
     left = lax.ppermute(tail, "lon", [(i, (i + 1) % lon) for i in range(lon)])
     right = lax.ppermute(head, "lon", [((i + 1) % lon, i) for i in range(lon)])
 
-    def widened(index, block):
-        tail = jnp.zeros((ROWS, width + MARGIN - cols - 2 * wide, block.shape[2]), BF16)
-        return jnp.concatenate([left[index], block, right[index], tail], axis=1)
-
-    fields_halo = exchanged(widened(0, activ))
-    cot_wide = widened(1, cot)
-    cot_halo = exchanged(cot_wide)
+    rims = exchanged(jnp.concatenate([left, right], axis=2))
+    tail = jnp.zeros((ROWS, width + MARGIN - cols - 2 * wide, activ.shape[2]), BF16)
+
+    def widened(index, blocks):
+        return tuple(
+            jnp.concatenate([rim[index, :, :wide], block, rim[index, :, wide:], tail], axis=1)
+            for rim, block in zip(rims, blocks)
+        )
+
+    fields_own = exchanged(activ)
+    later, fields_own, rims = lax.optimization_barrier((cot, fields_own, rims))
+    fields_halo = widened(0, fields_own)
+    cot_parts = exchanged(later)
 
     pull_one, push_one = filter_tables(masked_filters(filter_one, band_width), source_rows, first_row)
     pull_two, push_two = filter_tables(masked_filters(filter_two, band_width), source_rows, first_row)
 
     hidden, slope = layer("gate", cols, fields_halo, pull_one, mix_one)
     hidden_halo = exchanged(hidden)
+    cot_parts, rims, slope = lax.optimization_barrier((cot_parts, rims, slope))
+    cot_halo = widened(1, cot_parts)
     (pre_grad,) = layer("scale", cols, cot_halo, push_two, mix_two, turn=True, slope=slope)
     pre_halo = exchanged(pre_grad)
     inner = (WHALF, WHALF + cols)
+    factor = float(1.0 / np.sqrt(np.float32(total_rows * total_cols * lax.axis_size("ens"))))
     (part_one,) = layer("none", cols, fields_halo, pull_one, grad=pre_grad, valid=inner)
-    forward, part_two = layer("plain", cols, hidden_halo, pull_two, mix_two, grad=cot, valid=(0, cols))
-    factor = float(1.0 / np.sqrt(np.float32(total_rows * total_cols * lax.axis_size("ens"))))
-    adjoint, sums = layer(
-        "plain", cols, pre_halo, push_one, mix_one, turn=True, parts=[part_one, part_two], scale=factor
+    forward, sum_one, part_two = layer(
+        "plain", cols, hidden_halo, pull_two, mix_two, grad=cot, valid=(0, cols), parts=[part_one], scale=factor
     )
-    sums = sums.astype(F32)
-    length = part_one.shape[0]
-    total_one, total_two = sums[:length], sums[length : 2 * length]
+    adjoint, sum_two = layer(
+        "plain", cols, pre_halo, push_one, mix_one, turn=True, parts=[part_two], scale=factor, ident=1
+    )
+    total_one = sum_one[: part_one.shape[0]].astype(F32)
+    total_two = sum_two[: part_two.shape[0]].astype(F32)
     return forward[None], adjoint[None], total_one, total_two
 
 

time: 159 us -> 168 us (1.057)
  starting transfers between devices: 23.4 us -> 32.6 us
  local copies, waits for them, and re-layouts: 25.5 us -> 19.8 us
  waiting for transfers between devices: 6.61 us -> 1.53 us
  other arithmetic: 4.95 us -> 9.97 us
  Pallas kernels: 94.2 us -> 97.1 us
  matrix products: 2.49 us -> 4.66 us
    ppermute x4 -> x5, starting transfers between devices: 15.2 us -> 23.7 us  [exchanged(): up = lax.ppermute(block, 'lat', [(i, i + 1) for i in range(count - 1)])]
    ppermute x4 -> x5, waiting for transfers between devices: 6.6 us -> 1.51 us  [exchanged(): down = lax.ppermute(block, 'lat', [(i + 1, i) for i in range(count - 1)])]
    reshape x4, local copies, waits for them, and re-layouts: 9.91 us -> 4.93 us  [banded(): return out.astype(BF16).reshape(ROWS, K * TILE, NEAR * SPAN)]
    concatenate x1 -> x2, other arithmetic: 0.46 us -> 5.31 us  [widened(): jnp.concatenate([rim[index, :, :wide], block, rim[index, :, wide:], tail]...]
    pallas_call x5, Pallas kernels: 94.2 us -> 97.1 us  [layer(): pl.pallas_call(functools.partial(layer_kernel, mode, width, cols, turn, v...]
    squeeze x2 -> x5, local copies, waits for them, and re-layouts: 0.01 us -> 2.92 us  [widened(): rim[index, :, :wide]]
    dot_general x4, matrix products: 1.96 us -> 4.12 us  [banded(): jnp.einsum('rekw,wtv->rktev', table, chosen, preferred_element_type=F32)]
    convert_element_type x4, local copies, waits for them, and re-layouts: 5.39 us -> 3.36 us  [banded(): return out.astype(BF16).reshape(ROWS, K * TILE, NEAR * SPAN)]
  transfers between devices with their start and end apart: 10 -> 12, of which waited for: 2 -> 1; matrix products, arithmetic and copies ran while one was open for 17% -> 18% of each run, Pallas kernels for 40% -> 43%
where the time goes in v3:
time: 168 us; the launch traced here: 167 us
  Pallas kernels  97.1 us (58%)
  starting transfers between devices  32.6 us (19%)
  local copies, waits for them, and re-layouts  19.8 us (12%)
  other arithmetic  9.97 us (6%)
  matrix products  4.66 us (3%)
    pallas_call x5, Pallas kernels, layer(): pl.pallas_call(functools.partial(layer_kernel, mode, width, cols, turn, v...  97.1 us
    ppermute x5, starting transfers between devices, exchanged(): up = lax.ppermute(block, 'lat', [(i, i + 1) for i in range(count - 1)])  23.7 us
    ppermute x5, starting transfers between devices, exchanged(): down = lax.ppermute(block, 'lat', [(i + 1, i) for i in range(count - 1)])  6.84 us
    concatenate x2, other arithmetic, widened(): jnp.concatenate([rim[index, :, :wide], block, rim[index, :, wide:], tail]...  5.31 us
    unnamed x18, local copies, waits for them, and re-layouts  5.06 us
    reshape x4, local copies, waits for them, and re-layouts, banded(): return out.astype(BF16).reshape(ROWS, K * TILE, NEAR * SPAN)  4.93 us
    dot_general x4, matrix products, banded(): jnp.einsum('rekw,wtv->rktev', table, chosen, preferred_element_type=F32)  4.12 us
  transfers between devices with their start and end apart: 12, of which 1 were waited for; matrix products, arithmetic and copies ran while one was open for 18% of the time, Pallas kernels for 43%

profile of v3, /device:TPU:0, one launch (start us, length us, event | category | flops | bytes accessed | tf_op | source)
XLA Modules:
  0.0 166.7 jit_solution(18036661950209763556)
XLA Ops:
  0.6 6.0 %collective-permute-start = (bf16[2,720,384]{2,1,0:T(8,128)(2,1)}, bf16[2,720,384]{2,1,0:T(8,128)(2,1)}, u32[]{:S(2)}, u32[]{:S(2)}) collective-permute-start(bf16[2,720,384]{2,1,0:T(8,128)(2,1)} %bitcast.92), channel_id=1, source_target_pairs={{0,4},{4,8},{8,12},{1,5},{5,9},{9,13},{2,6},{6,10},{10,14},{3,7},{... | collective-permute-start | bytes 3317768 | tf_op jit(solution)/shard_map/ppermute | solution.py:212
  9.4 1.6 collective-permute-start.2
  15.5 1.4 fusion.33
  18.6 1.6 fusion.1
  20.3 5.2 %collective-permute-start.4 = (bf16[2,2,16,384]{3,2,1,0:T(8,128)(2,1)S(1)}, bf16[2,2,16,384]{3,2,1,0:T(8,128)(2,1)}, u32[]{:S(2)}, u32[]{:S(2)}) collective-permute-start(bf16[2,2,16,384]{3,2,1,0:T(8,128)(2,1)S(1)} %constant_dynamic-update-slice_fusion), channel_id=1, source_target_pairs={{0,4},{4,8},{8,12},{1,5},{5,9},{9,13},{2,6},{6,10},{10,14},{3,7},{... | collective-permute-start | bytes 147464 | tf_op jit(solution)/shard_map/ppermute | solution.py:212
  26.8 1.6 fusion.3
  28.4 1.4 copy.41
  29.7 1.8 %reshape.74.refs_3_ = bf16[2,288,240]{2,1,0:T(8,128)(2,1)S(1)} reshape(bf16[2,9,32,5,48]{4,3,2,1,0:T(8,128)(2,1)} %copy.41) | data formatting | bytes 552960 | tf_op jit(solution)/shard_map/reshape | solution.py:229
  31.6 1.4 copy.49
  33.0 2.0 %reshape.76.refs_3_ = bf16[2,288,240]{2,1,0:T(8,128)(2,1)S(1)} reshape(bf16[2,9,32,5,48]{4,3,2,1,0:T(8,128)(2,1)} %copy.49) | data formatting | bytes 552960 | tf_op jit(solution)/shard_map/reshape | solution.py:229
  38.2 4.6 %collective-permute-start.8 = (bf16[2,720,384]{2,1,0:T(8,128)(2,1)S(1)}, bf16[2,720,384]{2,1,0:T(8,128)(2,1)S(1)}, u32[]{:S(2)}, u32[]{:S(2)}) collective-permute-start(bf16[2,720,384]{2,1,0:T(8,128)(2,1)S(1)} %bitcast.86), channel_id=1, source_target_pairs={{0,4},{4,8},{8,12},{1,5},{5,9},{9,13},{2,6},{6,10},{10,14},{3,7},{... | collective-permute-start | bytes 3317768 | tf_op jit(solution)/shard_map/ppermute | solution.py:212
  42.8 1.5 collective-permute-start.9
  45.7 3.4 %maximum_maximum_fusion.2 = (bf16[2,752,384]{2,1,0:T(8,128)(2,1)S(1)}, bf16[2,752,384]{2,1,0:T(8,128)(2,1)S(1)}, bf16[2,752,384]{2,1,0:T(8,128)(2,1)S(1)}) fusion(bf16[2,8,384]{2,1,0:T(8,128)(2,1)S(1)} %get-tuple-element.63, bf16[2,720,384]{2,1,0:T(8,128)(2,1)} %collective-permute-done.1, bf16[2,8,384]{2,1,0:T(8,128)(2,1)S(1)} %get-tuple-element.62, ...), kind=kLoop, calls=%fused_computation.10 | loop fusion | flops 12705792 | bytes 6858208 | tf_op jit(solution)/shard_map/concatenate | solution.py:365
  49.1 12.8 %shard_map.111 = (bf16[2,752,384]{2,1,0:T(8,128)(2,1)S(1)}, f32[2,736,384]{2,1,0:T(8,128)}) custom-call(bf16[2,752,384]{2,1,0:T(8,128)(2,1)S(1)} %get-tuple-element.77.refs_0_, bf16[2,752,384]{2,1,0:T(8,128)(2,1)S(1)} %get-tuple-element.76.refs_1_, bf16[2,752,384]{2,1,0:T(8,128)(2,1)S(1)} %get-tuple-element.75.refs_2_, ...), custom_call_target="tpu_custom_call" | custom-call | flops 6945767424 | bytes 10485760 | tf_op jit(solution)/shard_map/pallas_call | solution.py:199
  61.9 4.6 %collective-permute-start.6 = (bf16[2,752,384]{2,1,0:T(8,128)(2,1)S(1)}, bf16[2,752,384]{2,1,0:T(8,128)(2,1)S(1)}, u32[]{:S(2)}, u32[]{:S(2)}) collective-permute-start(bf16[2,752,384]{2,1,0:T(8,128)(2,1)S(1)} %get-tuple-element.31.refs_1_), channel_id=1, source_target_pairs={{0,4},{4,8},{8,12},{1,5},{5,9},{9,13},{2,6},{6,10},{10,14},{3,7},{... | collective-permute-start | bytes 3465224 | tf_op jit(solution)/shard_map/ppermute | solution.py:212
  66.5 1.3 collective-permute-start.7
  67.8 1.5 collective-permute-done.9
  70.8 1.9 %maximum_maximum_fusion.5 = (bf16[2,752,384]{2,1,0:T(8,128)(2,1)S(1)}, bf16[2,752,384]{2,1,0:T(8,128)(2,1)S(1)}, bf16[2,752,384]{2,1,0:T(8,128)(2,1)S(1)}) fusion(bf16[2,8,384]{2,1,0:T(8,128)(2,1)S(1)} %get-tuple-element.57, bf16[2,720,384]{2,1,0:T(8,128)(2,1)S(1)} %collective-permute-done.9, bf16[2,8,384]{2,1,0:T(8,128)(2,1)S(1)} %get-tuple-element.56, ...), kind=kLoop, calls=%fused_computation.13 | loop fusion | flops 12705792 | bytes 6858208 | tf_op jit(solution)/shard_map/concatenate | solution.py:365
  72.7 14.2 %shard_map.112.refs_4_.refs_1_ = bf16[2,752,384]{2,1,0:T(8,128)(2,1)S(1)} custom-call(bf16[2,752,384]{2,1,0:T(8,128)(2,1)S(1)} %get-tuple-element.73.refs_0_, bf16[2,752,384]{2,1,0:T(8,128)(2,1)S(1)} %get-tuple-element.74.refs_1_, bf16[2,752,384]{2,1,0:T(8,128)(2,1)S(1)} %get-tuple-element.72.refs_2_, bf16[2,288,240]{2,1,0:T(8,128)(2,1)S(1)} %reshape.76.refs_3_, ...), custom_call_target="tpu_custom_call" | custom-call | flops 6945767424 | bytes 10485760 | tf_op jit(solution)/shard_map/pallas_call | solution.py:199
  87.0 3.3 %collective-permute-start.10 = (bf16[2,752,384]{2,1,0:T(8,128)(2,1)S(1)}, bf16[2,752,384]{2,1,0:T(8,128)(2,1)S(1)}, u32[]{:S(2)}, u32[]{:S(2)}) collective-permute-start(bf16[2,752,384]{2,1,0:T(8,128)(2,1)S(1)} %shard_map.112.refs_4_.refs_1_), channel_id=1, source_target_pairs={{0,4},{4,8},{8,12},{1,5},{5,9},{9,13},{2,6},{6,10},{10,14},{3,7},{... | collective-permute-start | bytes 3465224 | tf_op jit(solution)/shard_map/ppermute | solution.py:212
  90.2 1.5 collective-permute-start.11
  91.8 14.1 %shard_map.113.refs_5_ = f32[432,384]{1,0:T(8,128)S(1)} custom-call(bf16[2,752,384]{2,1,0:T(8,128)(2,1)S(1)} %get-tuple-element.77.refs_0_, bf16[2,752,384]{2,1,0:T(8,128)(2,1)S(1)} %get-tuple-element.76.refs_1_, bf16[2,752,384]{2,1,0:T(8,128)(2,1)S(1)} %get-tuple-element.75.refs_2_, bf16[2,288,240]{2,1,0:T(8,128)(2,1)S(1)} %reshape.74.refs_3_, ...), custom_call_target="tpu_custom_call" | custom-call | flops 6945767424 | bytes 10485760 | tf_op jit(solution)/shard_map/pallas_call | solution.py:199
  105.9 31.2 %shard_map.114 = (bf16[2,720,384]{2,1,0:T(8,128)(2,1)S(1)}, bf16[512,384]{1,0:T(8,128)(2,1)S(1)}, f32[432,384]{1,0:T(8,128)S(1)}) custom-call(bf16[2,752,384]{2,1,0:T(8,128)(2,1)S(1)} %collective-permute-done.6.refs_0_, bf16[2,752,384]{2,1,0:T(8,128)(2,1)} %copy-done.1, bf16[2,752,384]{2,1,0:T(8,128)(2,1)} %collective-permute-done.7.refs_2_, ...), custom_call_target="tpu_custom_call" | custom-call | flops 10418651136 | bytes 10485760 | tf_op jit(solution)/shard_map/pallas_call | solution.py:199
  139.1 24.7 %shard_map.115 = (bf16[2,720,384]{2,1,0:T(8,128)(2,1)S(1)}, bf16[512,384]{1,0:T(8,128)(2,1)S(1)}) custom-call(bf16[2,752,384]{2,1,0:T(8,128)(2,1)S(1)} %collective-permute-done.10.refs_0_, bf16[2,752,384]{2,1,0:T(8,128)(2,1)S(1)} %shard_map.112.refs_4_.refs_1_, bf16[2,752,384]{2,1,0:T(8,128)(2,1)} %copy-done.6, bf16[2,288,240]{2,1,0:T(8,128)(2,1)S(1)} %reshape.77.refs_3_, ...), custom_call_target="tpu_custom_call" | custom-call | flops 6945767424 | bytes 10485760 | tf_op jit(solution)/shard_map/pallas_call | solution.py:199
  (74 shorter events, 21.3 us)
Async XLA Ops:
  0.6 37.0 %collective-permute-start = (bf16[2,720,384]{2,1,0:T(8,128)(2,1)}, bf16[2,720,384]{2,1,0:T(8,128)(2,1)}, u32[]{:S(2)}, u32[]{:S(2)}) collective-permute-start(bf16[2,720,384]{2,1,0:T(8,128)(2,1)} %bitcast.92), channel_id=1, source_target_pairs={{0,4},{4,8},{8,12},{1,5},{5,9},{9,13},{2,6},{6,10},{10,14},{3,7},{... | collective-permute-start | bytes 3317768 | tf_op jit(solution)/shard_map/ppermute | solution.py:212
  6.6 31.0 %collective-permute-start.1 = (bf16[2,720,384]{2,1,0:T(8,128)(2,1)}, bf16[2,720,384]{2,1,0:T(8,128)(2,1)}, u32[]{:S(2)}, u32[]{:S(2)}) collective-permute-start(bf16[2,720,384]{2,1,0:T(8,128)(2,1)} %bitcast.93), channel_id=1, source_target_pairs={{4,0},{8,4},{12,8},{5,1},{9,5},{13,9},{6,2},{10,6},{14,10},{7,3},{... | collective-permute-start | bytes 3317768 | tf_op jit(solution)/shard_map/ppermute | solution.py:213
  9.4 10.9 %collective-permute-start.2 = (bf16[2,2,8,384]{3,2,1,0:T(8,128)(2,1)S(1)}, bf16[2,2,8,384]{3,2,1,0:T(8,128)(2,1)S(1)}, u32[]{:S(2)}, u32[]{:S(2)}) collective-permute-start(bf16[2,2,8,384]{3,2,1,0:T(8,128)(2,1)S(1)} %pad_maximum_fusion), channel_id=1, source_target_pairs={{0,2},{2,0},{1,3},{3,1},{4,6},{6,4},{5,7},{7,5},{8,10},{10,8},{9,1... | collective-permute-start | bytes 73736 | tf_op jit(solution)/shard_map/ppermute | solution.py:357
  10.9 9.4 %collective-permute-start.3 = (bf16[2,2,8,384]{3,2,1,0:T(8,128)(2,1)S(1)}, bf16[2,2,8,384]{3,2,1,0:T(8,128)(2,1)S(1)}, u32[]{:S(2)}, u32[]{:S(2)}) collective-permute-start(bf16[2,2,8,384]{3,2,1,0:T(8,128)(2,1)S(1)} %pad_maximum_fusion.1), channel_id=1, source_target_pairs={{2,0},{0,2},{3,1},{1,3},{6,4},{4,6},{7,5},{5,7},{10,8},{8,10},{11,... | collective-permute-start | bytes 73736 | tf_op jit(solution)/shard_map/ppermute | solution.py:358
  20.3 17.2 %collective-permute-start.4 = (bf16[2,2,16,384]{3,2,1,0:T(8,128)(2,1)S(1)}, bf16[2,2,16,384]{3,2,1,0:T(8,128)(2,1)}, u32[]{:S(2)}, u32[]{:S(2)}) collective-permute-start(bf16[2,2,16,384]{3,2,1,0:T(8,128)(2,1)S(1)} %constant_dynamic-update-slice_fusion), channel_id=1, source_target_pairs={{0,4},{4,8},{8,12},{1,5},{5,9},{9,13},{2,6},{6,10},{10,14},{3,7},{... | collective-permute-start | bytes 147464 | tf_op jit(solution)/shard_map/ppermute | solution.py:212
  25.5 12.0 %collective-permute-start.5 = (bf16[2,2,16,384]{3,2,1,0:T(8,128)(2,1)S(1)}, bf16[2,2,16,384]{3,2,1,0:T(8,128)(2,1)}, u32[]{:S(2)}, u32[]{:S(2)}) collective-permute-start(bf16[2,2,16,384]{3,2,1,0:T(8,128)(2,1)S(1)} %constant_dynamic-update-slice_fusion), channel_id=1, source_target_pairs={{4,0},{8,4},{12,8},{5,1},{9,5},{13,9},{6,2},{10,6},{14,10},{7,3},{... | collective-permute-start | bytes 147464 | tf_op jit(solution)/shard_map/ppermute | solution.py:213
  33.0 2.0 %copy-start.4 = (bf16[2,9,32,5,48]{4,1,3,0,2:T(8,128)(2,1)S(1)}, bf16[2,9,32,5,48]{4,1,3,0,2:T(8,128)(2,1)}, u32[]{:S(2)}) copy-start(bf16[2,9,32,5,48]{4,1,3,0,2:T(8,128)(2,1)} %fusion.1) | copy-start | bytes 829444
  35.3 1.3 copy-start.5
  36.9 1.2 copy-start
  38.2 29.6 %collective-permute-start.8 = (bf16[2,720,384]{2,1,0:T(8,128)(2,1)S(1)}, bf16[2,720,384]{2,1,0:T(8,128)(2,1)S(1)}, u32[]{:S(2)}, u32[]{:S(2)}) collective-permute-start(bf16[2,720,384]{2,1,0:T(8,128)(2,1)S(1)} %bitcast.86), channel_id=1, source_target_pairs={{0,4},{4,8},{8,12},{1,5},{5,9},{9,13},{2,6},{6,10},{10,14},{3,7},{... | collective-permute-start | bytes 3317768 | tf_op jit(solution)/shard_map/ppermute | solution.py:212
  42.8 26.5 %collective-permute-start.9 = (bf16[2,720,384]{2,1,0:T(8,128)(2,1)S(1)}, bf16[2,720,384]{2,1,0:T(8,128)(2,1)S(1)}, u32[]{:S(2)}, u32[]{:S(2)}) collective-permute-start(bf16[2,720,384]{2,1,0:T(8,128)(2,1)S(1)} %bitcast.87), channel_id=1, source_target_pairs={{4,0},{8,4},{12,8},{5,1},{9,5},{13,9},{6,2},{10,6},{14,10},{7,3},{... | collective-permute-start | bytes 3317768 | tf_op jit(solution)/shard_map/ppermute | solution.py:213
  45.7 3.4 %copy-start.3 = (bf16[432,384]{1,0:T(8,128)(2,1)S(1)}, bf16[432,384]{1,0:T(8,128)(2,1)}, u32[]{:S(2)}) copy-start(bf16[432,384]{1,0:T(8,128)(2,1)} %refs_4_.7) | copy-start | bytes 995332
  61.9 10.8 %copy-start.1 = (bf16[2,752,384]{2,1,0:T(8,128)(2,1)}, bf16[2,752,384]{2,1,0:T(8,128)(2,1)S(1)}, u32[]{:S(2)}) copy-start(bf16[2,752,384]{2,1,0:T(8,128)(2,1)S(1)} %get-tuple-element.31.refs_1_) | copy-start | bytes 3465220
  61.9 44.0 %collective-permute-start.6 = (bf16[2,752,384]{2,1,0:T(8,128)(2,1)S(1)}, bf16[2,752,384]{2,1,0:T(8,128)(2,1)S(1)}, u32[]{:S(2)}, u32[]{:S(2)}) collective-permute-start(bf16[2,752,384]{2,1,0:T(8,128)(2,1)S(1)} %get-tuple-element.31.refs_1_), channel_id=1, source_target_pairs={{0,4},{4,8},{8,12},{1,5},{5,9},{9,13},{2,6},{6,10},{10,14},{3,7},{... | collective-permute-start | bytes 3465224 | tf_op jit(solution)/shard_map/ppermute | solution.py:212
  66.5 39.4 %collective-permute-start.7 = (bf16[2,752,384]{2,1,0:T(8,128)(2,1)S(1)}, bf16[2,752,384]{2,1,0:T(8,128)(2,1)}, u32[]{:S(2)}, u32[]{:S(2)}) collective-permute-start(bf16[2,752,384]{2,1,0:T(8,128)(2,1)S(1)} %get-tuple-element.31.refs_1_), channel_id=1, source_target_pairs={{4,0},{8,4},{12,8},{5,1},{9,5},{13,9},{6,2},{10,6},{14,10},{7,3},{... | collective-permute-start | bytes 3465224 | tf_op jit(solution)/shard_map/ppermute | solution.py:213
  70.8 1.9 %copy-start.2 = (bf16[432,384]{1,0:T(8,128)(2,1)S(1)}, bf16[432,384]{1,0:T(8,128)(2,1)}, u32[]{:S(2)}) copy-start(bf16[432,384]{1,0:T(8,128)(2,1)} %refs_4_.6) | copy-start | bytes 995332
  87.0 51.1 %collective-permute-start.10 = (bf16[2,752,384]{2,1,0:T(8,128)(2,1)S(1)}, bf16[2,752,384]{2,1,0:T(8,128)(2,1)S(1)}, u32[]{:S(2)}, u32[]{:S(2)}) collective-permute-start(bf16[2,752,384]{2,1,0:T(8,128)(2,1)S(1)} %shard_map.112.refs_4_.refs_1_), channel_id=1, source_target_pairs={{0,4},{4,8},{8,12},{1,5},{5,9},{9,13},{2,6},{6,10},{10,14},{3,7},{... | collective-permute-start | bytes 3465224 | tf_op jit(solution)/shard_map/ppermute | solution.py:212
  90.2 47.8 %collective-permute-start.11 = (bf16[2,752,384]{2,1,0:T(8,128)(2,1)S(1)}, bf16[2,752,384]{2,1,0:T(8,128)(2,1)S(1)}, u32[]{:S(2)}, u32[]{:S(2)}) collective-permute-start(bf16[2,752,384]{2,1,0:T(8,128)(2,1)S(1)} %shard_map.112.refs_4_.refs_1_), channel_id=1, source_target_pairs={{4,0},{8,4},{12,8},{5,1},{9,5},{13,9},{6,2},{10,6},{14,10},{7,3},{... | collective-permute-start | bytes 3465224 | tf_op jit(solution)/shard_map/ppermute | solution.py:213
  138.1 1.0 copy-start.6
